TPU v7x, 256 devices: a whole 4x4x8 slice. The times are simulated.
256 devices in a mesh: hi: 16 (over y, z_hi, core), lo: 16 (over z_lo, x).
Axes of the slice: x: 4, y: 4, z: 8 (z_hi: 2, z_lo: 4; z = z_hi * 4 + z_lo), core: 2. Of those that a mesh axis runs over, the one named last changes fastest.
Arguments:
- inputs: bfloat16 [131072, 192], P(('hi', 'lo')), may hold values from -6 to 6
- upstream: bfloat16 [131072, 192], P(('hi', 'lo')), may hold values from -6 to 6
- w_in: bfloat16 [768, 384], replicated, may hold values from -0.3125 to 0.3125
- w_out: bfloat16 [768, 384], replicated, may hold values from -0.21875 to 0.21875
- bias: float32 [768], replicated, may hold values from -4 to 4
Outputs:
- features_out: bfloat16 [131072, 192], P(('hi', 'lo'))
- grad_input: bfloat16 [131072, 192], P(('hi', 'lo'))
- grad_w_in: float32 [768, 384], P(('hi', 'lo'))
- grad_w_out: float32 [768, 384], P(('hi', 'lo'))
- grad_bias: float32 [768], P(('hi', 'lo'))
All inputs are finite; a program needn't handle non-finite values.
Results may differ from a plain program's by a relative error of at most 0.015.
Values may be sent and summed in bfloat16 or wider, within the bound.
No kernel may reach another device: no remote copies, remote signals or barrier semaphores. Data moves between devices by JAX's collectives and lax.ppermute only.
A program may use at most 64 MiB of HBM per device.

v0:
```python
import math

import jax
import jax.numpy as jnp
from jax import lax
from jax.sharding import PartitionSpec as P


def from_partner(block, axis, stride):
    count = lax.axis_size(axis)
    route = []
    for low in range(count):
        high = low | 1 << stride
        if high != low and high < count:
            route += [(low, high), (high, low)]
    return lax.ppermute(block, axis, route)


def bit_count(value):
    return value.bit_length() - 1


def gelu_pair(pre):
    coeff = math.sqrt(2.0 / math.pi)
    inner = coeff * (pre + 0.044715 * pre * pre * pre)
    tangent = jnp.tanh(inner)
    value = 0.5 * pre * (1.0 + tangent)
    deriv = 0.5 * (1.0 + tangent) + 0.5 * pre * (1.0 - tangent * tangent) * coeff * (
        1.0 + 3.0 * 0.044715 * pre * pre
    )
    return (value, deriv)


def normalize(paired):
    values = paired.astype(jnp.float32)
    centered = values - jnp.mean(values, axis=-1, keepdims=True)
    inverse = lax.rsqrt(jnp.mean(centered * centered, axis=-1, keepdims=True) + 1e-05)
    return (centered * inverse, inverse)


def unit_forward(paired, w_in, w_out, bias):
    nhat, inverse = normalize(paired)
    normed = nhat.astype(jnp.bfloat16)
    pre = (
        lax.dot_general(normed, w_in, (((1,), (1,)), ((), ())), preferred_element_type=jnp.float32)
        + bias
    )
    value, deriv = gelu_pair(pre)
    hidden = value.astype(jnp.bfloat16)
    branch = jnp.dot(hidden, w_out, preferred_element_type=jnp.float32)
    return (paired.astype(jnp.float32) + branch).astype(jnp.bfloat16)


def unit_backward(paired, grad_y, w_in, w_out, bias):
    nhat, inverse = normalize(paired)
    normed = nhat.astype(jnp.bfloat16)
    pre = (
        lax.dot_general(normed, w_in, (((1,), (1,)), ((), ())), preferred_element_type=jnp.float32)
        + bias
    )
    value, deriv = gelu_pair(pre)
    hidden = value.astype(jnp.bfloat16)
    grad_out = lax.dot_general(
        hidden, grad_y, (((0,), (0,)), ((), ())), preferred_element_type=jnp.float32
    )
    grad_hidden = lax.dot_general(
        grad_y, w_out, (((1,), (1,)), ((), ())), preferred_element_type=jnp.float32
    )
    grad_pre = grad_hidden * deriv
    grad_bias = jnp.sum(grad_pre, axis=0)
    grad_pre_b = grad_pre.astype(jnp.bfloat16)
    grad_in = lax.dot_general(
        grad_pre_b, normed, (((0,), (0,)), ((), ())), preferred_element_type=jnp.float32
    )
    grad_norm = jnp.dot(grad_pre_b, w_in, preferred_element_type=jnp.float32)
    grad_pair = grad_y.astype(jnp.float32) + inverse * (
        grad_norm
        - jnp.mean(grad_norm, axis=-1, keepdims=True)
        - nhat * jnp.mean(grad_norm * nhat, axis=-1, keepdims=True)
    )
    return (grad_pair.astype(jnp.bfloat16), grad_in, grad_out, grad_bias)


def join_pair(lower, mine, other):
    return jnp.where(
        lower, jnp.concatenate([mine, other], axis=1), jnp.concatenate([other, mine], axis=1)
    )


def on_device(inputs, upstream, w_in, w_out, bias):
    rows, width = inputs.shape
    devices = lax.axis_size(("hi", "lo"))
    lo_bits = bit_count(lax.axis_size("lo"))
    hi_bits = bit_count(lax.axis_size("hi"))
    shifts = [lo_bits + hi_bits - 1, lo_bits - 1, lo_bits, 0]
    position = lax.axis_index(("hi", "lo"))
    current = inputs
    saved = []
    sides = []
    for shift in shifts:
        side = jnp.bitwise_and(jnp.right_shift(position, shift), 1)
        lower = side == 0
        sides.append(side)
        other = from_partner(current, ("hi", "lo"), shift)
        paired = join_pair(lower, current, other)
        section_out = unit_forward(paired, w_in, w_out, bias)
        current = jnp.where(lower, section_out[:, :width], section_out[:, width:])
        saved.append(paired)
    grads = upstream
    weight_share = 0.5
    factor = 1.0 / math.sqrt(float(rows * devices))
    total_in = jnp.zeros(w_in.shape, jnp.float32)
    total_out = jnp.zeros(w_out.shape, jnp.float32)
    total_bias = jnp.zeros(bias.shape, jnp.float32)
    for section in range(len(shifts) - 1, -1, -1):
        shift = shifts[section]
        side = sides[section]
        lower = side == 0
        other = from_partner(grads, ("hi", "lo"), shift)
        grad_y = join_pair(lower, grads, other)
        grad_pair, part_in, part_out, part_bias = unit_backward(
            saved[section], grad_y, w_in, w_out, bias
        )
        grads = jnp.where(lower, grad_pair[:, :width], grad_pair[:, width:])
        total_in = total_in + part_in
        total_out = total_out + part_out
        total_bias = total_bias + part_bias
    share_in, share_out, share_bias = (
        lax.psum_scatter(total_in * weight_share, ("hi", "lo"), scatter_dimension=0, tiled=True),
        lax.psum_scatter(total_out * weight_share, ("hi", "lo"), scatter_dimension=0, tiled=True),
        lax.psum_scatter(total_bias * weight_share, ("hi", "lo"), scatter_dimension=0, tiled=True),
    )
    return (current, grads, share_in * factor, share_out * factor, share_bias * factor)


def solution(mesh):
    in_specs = (P(("hi", "lo"), None), P(("hi", "lo"), None), P(), P(), P())
    out_specs = (
        P(("hi", "lo"), None),
        P(("hi", "lo"), None),
        P(("hi", "lo"), None),
        P(("hi", "lo"), None),
        P(("hi", "lo")),
    )
    return jax.shard_map(
        on_device, mesh=mesh, in_specs=in_specs, out_specs=out_specs, check_vma=False
    )
```

profile of v0, /device:TPU:2, one launch (start us, length us, event | category | flops | bytes accessed | tf_op | source)
XLA Modules:
  0.0 435.0 jit_solution(13649595400228455579)
XLA Ops:
  7.2 3.3 collective-permute-start
  10.5 5.2 %collective-permute-done = bf16[512,192]{0,1:T(8,128)(2,1)S(1)} collective-permute-done((bf16[512,192]{0,1:T(8,128)(2,1)}, bf16[512,192]{0,1:T(8,128)(2,1)S(1)}, u32[]{:S(2)}, u32[]{:S(2)}) %collective-permute-start) | collective-permute-done | bytes 196640 | tf_op jit(solution)/shard_map/ppermute | solution.py:16
  15.7 1.2 convert_reduce_fusion.3
  16.9 1.2 fusion.75
  18.1 1.7 convolution_add_fusion.3
  19.9 0.8 fusion.28
  21.1 3.4 collective-permute-start.1
  24.4 8.2 %collective-permute-done.1 = bf16[512,192]{0,1:T(8,128)(2,1)S(1)} collective-permute-done((bf16[512,192]{0,1:T(8,128)(2,1)S(1)}, bf16[512,192]{0,1:T(8,128)(2,1)S(1)}, u32[]{:S(2)}, u32[]{:S(2)}) %collective-permute-start.1) | collective-permute-done | bytes 196640 | tf_op jit(solution)/shard_map/ppermute | solution.py:16
  33.7 0.8 fusion.29
  34.9 1.4 collective-permute-done.2
  37.4 0.8 fusion.30
  39.2 1.5 collective-permute-start.4
  40.6 5.7 %collective-permute-done.3 = bf16[512,192]{0,1:T(8,128)(2,1)S(1)} collective-permute-done((bf16[512,192]{0,1:T(8,128)(2,1)S(1)}, bf16[512,192]{0,1:T(8,128)(2,1)S(1)}, u32[]{:S(2)}, u32[]{:S(2)}) %collective-permute-start.3) | collective-permute-done | bytes 196640 | tf_op jit(solution)/shard_map/ppermute | solution.py:16
  47.4 2.4 collective-permute-done.4
  49.8 1.2 fusion.106
  52.3 0.8 fusion.31
  54.6 1.2 fusion.107
  57.6 1.9 fusion.99
  59.4 9.9 %collective-permute-done.6 = bf16[512,192]{0,1:T(8,128)(2,1)S(1)} collective-permute-done((bf16[512,192]{0,1:T(8,128)(2,1)S(1)}, bf16[512,192]{0,1:T(8,128)(2,1)S(1)}, u32[]{:S(2)}, u32[]{:S(2)}) %collective-permute-start.6) | collective-permute-done | bytes 196640 | tf_op jit(solution)/shard_map/ppermute | solution.py:16
  69.3 1.2 fusion.105
  71.6 3.3 collective-permute-start.7
  75.6 1.8 fusion.98
  77.4 2.3 collective-permute-done.7
  79.7 2.1 fusion.104
  81.9 77.6 %all-reduce.2 = f32[768]{0:T(1024)S(1)} all-reduce(f32[768]{0:T(1024)S(1)} %add_multiply_fusion), channel_id=4, replica_groups=mesh['hi'=16,'lo'=16] {'hi','lo'}, use_global_device_ids=true, to_apply=%region_22.23.clone | all-reduce | flops 768 | bytes 6144
  160.1 2.3 fusion.97
  162.5 1.6 fusion.27
  164.7 2.0 fusion.26
  166.7 1.1 copy-done.13
  169.6 255.9 %all-reduce.6.cloned.1.call-done = (f32[768,384]{1,0:T(8,128)}, f32[768,384]{1,0:T(8,128)}) async-done(((f32[768,384]{1,0:T(8,128)}, f32[768,384]{1,0:T(8,128)}), (f32[768,384]{1,0:T(8,128)}, f32[768,384]{1,0:T(8,128)})) %all-reduce.6.cloned.1.call-update) | async-done | bytes 2359312
  425.5 1.3 dynamic-slice_multiply_fusion.1
  426.8 1.3 dynamic-slice_multiply_fusion
  (91 shorter events, 13.8 us)
Async XLA Ops:
  7.2 11.0 %copy-start = (bf16[768,384]{1,0:T(8,128)(2,1)S(1)}, bf16[768,384]{1,0:T(8,128)(2,1)}, u32[]{:S(2)}) copy-start(bf16[768,384]{1,0:T(8,128)(2,1)} %param.7) | copy-start | bytes 1769476
  7.2 418.3 %all-reduce.6.cloned.1.call-start = ((), (), s32[]{:S(2)}) async-start(), calls=%async_computation | async-start | bytes 4718592
  7.2 8.4 %collective-permute-start = (bf16[512,192]{0,1:T(8,128)(2,1)}, bf16[512,192]{0,1:T(8,128)(2,1)S(1)}, u32[]{:S(2)}, u32[]{:S(2)}) collective-permute-start(bf16[512,192]{0,1:T(8,128)(2,1)} %param.5), channel_id=1, source_target_pairs={{0,128},{128,0},{1,129},{129,1},{2,130},{130,2},{3,131},{131,3},{4... | collective-permute-start | bytes 589832 | tf_op jit(solution)/shard_map/ppermute | solution.py:16
  18.1 1.7 copy-start.1
  18.1 1.7 copy-start.5
  19.9 1.2 copy-start.14
  19.9 13.1 %copy-start.7 = (f32[768]{0:T(1024)S(1)}, f32[768]{0:T(1024)}, u32[]{:S(2)}) copy-start(f32[768]{0:T(1024)} %param.9) | copy-start | bytes 9220
  21.1 11.6 %collective-permute-start.1 = (bf16[512,192]{0,1:T(8,128)(2,1)S(1)}, bf16[512,192]{0,1:T(8,128)(2,1)S(1)}, u32[]{:S(2)}, u32[]{:S(2)}) collective-permute-start(bf16[512,192]{0,1:T(8,128)(2,1)S(1)} %slice_select_fusion.7), channel_id=1, source_target_pairs={{0,8},{8,0},{1,9},{9,1},{2,10},{10,2},{3,11},{11,3},{4,12},{12,4},... | collective-permute-start | bytes 589832 | tf_op jit(solution)/shard_map/ppermute | solution.py:16
  33.7 1.1 copy-start.16
  34.8 1.5 collective-permute-start.2
  37.3 1.2 copy-start.18
  37.3 1.8 copy-start.2
  38.5 7.8 %collective-permute-start.3 = (bf16[512,192]{0,1:T(8,128)(2,1)S(1)}, bf16[512,192]{0,1:T(8,128)(2,1)S(1)}, u32[]{:S(2)}, u32[]{:S(2)}) collective-permute-start(bf16[512,192]{0,1:T(8,128)(2,1)S(1)} %slice_select_fusion.5), channel_id=1, source_target_pairs={{0,1},{1,0},{2,3},{3,2},{4,5},{5,4},{6,7},{7,6},{8,9},{9,8},{10,11... | collective-permute-start | bytes 589832 | tf_op jit(solution)/shard_map/ppermute | solution.py:16
  39.2 10.6 %collective-permute-start.4 = (bf16[512,192]{0,1:T(8,128)(2,1)S(1)}, bf16[512,192]{0,1:T(8,128)(2,1)S(1)}, u32[]{:S(2)}, u32[]{:S(2)}) collective-permute-start(bf16[512,192]{0,1:T(8,128)(2,1)S(1)} %copy-done.2), channel_id=1, source_target_pairs={{0,1},{1,0},{2,3},{3,2},{4,5},{5,4},{6,7},{7,6},{8,9},{9,8},{10,11... | collective-permute-start | bytes 589832 | tf_op jit(solution)/shard_map/ppermute | solution.py:16
  47.4 5.0 %copy-start.8 = (f32[512,768]{1,0:T(8,128)}, f32[512,768]{1,0:T(8,128)S(1)}, u32[]{:S(2)}) copy-start(f32[512,768]{1,0:T(8,128)S(1)} %convolution_add_fusion) | copy-start | bytes 4718596
  49.8 1.8 copy-start.3
  52.1 2.4 collective-permute-start.5
  53.2 1.4 copy-start.19
  56.8 12.5 %collective-permute-start.6 = (bf16[512,192]{0,1:T(8,128)(2,1)S(1)}, bf16[512,192]{0,1:T(8,128)(2,1)S(1)}, u32[]{:S(2)}, u32[]{:S(2)}) collective-permute-start(bf16[512,192]{0,1:T(8,128)(2,1)S(1)} %slice_select_fusion.2), channel_id=1, source_target_pairs={{0,8},{8,0},{1,9},{9,1},{2,10},{10,2},{3,11},{11,3},{4,12},{12,4},... | collective-permute-start | bytes 589832 | tf_op jit(solution)/shard_map/ppermute | solution.py:16
  57.6 11.8 %copy-start.17 = (f32[512,768]{1,0:T(8,128)S(1)}, f32[512,768]{1,0:T(8,128)}, u32[]{:S(2)}) copy-start(f32[512,768]{1,0:T(8,128)} %copy-done.16) | copy-start | bytes 4718596
  71.6 8.1 %collective-permute-start.7 = (bf16[512,192]{0,1:T(8,128)(2,1)S(1)}, bf16[512,192]{0,1:T(8,128)(2,1)S(1)}, u32[]{:S(2)}, u32[]{:S(2)}) collective-permute-start(bf16[512,192]{0,1:T(8,128)(2,1)S(1)} %slice_select_fusion.1), channel_id=1, source_target_pairs={{0,128},{128,0},{1,129},{129,1},{2,130},{130,2},{3,131},{131,3},{4... | collective-permute-start | bytes 589832 | tf_op jit(solution)/shard_map/ppermute | solution.py:16
  75.6 4.2 copy-start.6
  75.6 4.2 copy-start.15
  160.1 2.4 copy-start.12
  160.1 4.0 copy-start.11
  162.4 1.7 copy-start.4
  162.4 1.7 copy-start.9
  162.5 2.3 copy-start.10
  166.7 1.1 copy-start.13
Sparse Core Ops, SparseCore 0:
  166.9 258.5 all-reduce.5
where the time goes:
time: 435 us
  waiting for transfers between devices  291 us (67%)
  blocking collectives  77.6 us (18%)
  matrix products  26.5 us (6%)
  between operations  14.5 us (3%)
  starting transfers between devices  12.5 us (3%)
  other arithmetic  9.97 us (2%)
    unnamed x2, waiting for transfers between devices  256 us
    unnamed x1, blocking collectives  77.6 us
    ppermute x8, waiting for transfers between devices, from_partner(): return lax.ppermute(block, axis, route)  35.2 us
    ppermute x8, starting transfers between devices, from_partner(): return lax.ppermute(block, axis, route)  12.5 us
  transfers between devices with their start and end apart: 9, of which 8 were waited for; matrix products, arithmetic and copies ran while one was open for 2% of the time, Pallas kernels for 0%

commit v1 on v0

v1 whole, which is shorter than its diff:
```python
import math

import jax
import jax.numpy as jnp
from jax import lax
from jax.experimental import pallas as pl
from jax.experimental.pallas import tpu as pltpu
from jax.sharding import Mesh
from jax.sharding import PartitionSpec as P

BITS = ("y1", "y0", "zh", "core", "zl1", "zl0", "x1", "x0")
SECTION_GROUP = ("y1", "core", "zl1", "x0")
PLANE_GROUP = ("y1", "y0", "x1", "x0")
COLUMN_GROUP = ("zh", "zl1", "zl0")
HIDDEN, WIDTH, PAIR = 768, 192, 384
QUARTER = 48
CHUNK = 256
BF16, F32 = jnp.bfloat16, jnp.float32
VMEM_LIMIT = 56 * 1024 * 1024


def swap_groups(parts):
    lane = lax.broadcasted_iota(jnp.int32, parts[0].shape, 1)
    for stride, at in ((2, 64), (1, 32)):
        low = (lane & at) == 0
        out = list(parts)
        for i in range(4):
            if not i & stride:
                a, b = parts[i], parts[i | stride]
                out[i] = jnp.where(low, a, pltpu.roll(b, at, 1))
                out[i | stride] = jnp.where(low, pltpu.roll(a, 128 - at, 1), b)
        parts = out
    return parts


def quarters(tile):
    return [tile[QUARTER * q : QUARTER * (q + 1)] for q in range(4)]


def group_of(y1, core, zl1, x0):
    return 8 * y1 + 4 * core + 2 * zl1 + x0


def pack_kernel(x_ref, g_ref, out_ref):
    for at, ref in enumerate((x_ref, g_ref)):
        for t in range(4):
            tile = ref[:, 128 * t : 128 * (t + 1)].astype(F32)
            for g, part in enumerate(swap_groups(quarters(tile))):
                out_ref[4 * t + g, QUARTER * at : QUARTER * (at + 1), :] = part.astype(BF16)


def unpack_kernel(in_ref, f_ref, g_ref):
    for at, ref in enumerate((f_ref, g_ref)):
        for t in range(4):
            parts = [
                in_ref[4 * t + g, QUARTER * at : QUARTER * (at + 1), :].astype(F32) for g in range(4)
            ]
            for q, part in enumerate(swap_groups(parts)):
                ref[QUARTER * q : QUARTER * (q + 1), 128 * t : 128 * (t + 1)] = part.astype(BF16)


def order_kernel(core_ref, w_in_ref, w_out_ref, bias_ref, win_ref, wint_ref, wout_ref, woutt_ref, b_ref):
    core = core_ref[0]

    def place(unit):
        device = (unit * 21846) >> 16
        third = unit - 3 * device
        block = (device >> 6) * 4 + (device & 3)
        z = ((device >> 5) & 1) * 4 + ((device >> 2) & 3)
        return (((device >> 4) & 1) ^ core) * (HIDDEN // 2) + block * 24 + third * 8 + z

    shape = (HIDDEN, HIDDEN)
    hit = lax.broadcasted_iota(jnp.int32, shape, 0) == place(lax.broadcasted_iota(jnp.int32, shape, 1))
    pick = hit.astype(F32).astype(BF16)
    for ref, out, out_t in ((w_in_ref, win_ref, wint_ref), (w_out_ref, wout_ref, woutt_ref)):
        moved = jnp.dot(pick, ref[...], preferred_element_type=F32)
        out[...] = moved.astype(BF16)
        out_t[...] = moved.T.astype(BF16)
    moved = jnp.sum(jnp.where(hit, bias_ref[...], 0.0), axis=1, keepdims=True)
    b_ref[...] = jnp.broadcast_to(moved, (HIDDEN, 128))


def gelu_pair(pre):
    coeff = math.sqrt(2.0 / math.pi)
    square = pre * pre
    tangent = jnp.tanh(coeff * pre * (1.0 + 0.044715 * square))
    half = 0.5 * (1.0 + tangent)
    value = pre * half
    deriv = half + 0.5 * coeff * pre * (1.0 - tangent * tangent) * (1.0 + 3.0 * 0.044715 * square)
    return value, deriv


def pair_tiles(tiles, bit):
    other = 3 - bit
    return jnp.concatenate(
        [
            jnp.concatenate([tiles[0], tiles[other]], axis=1),
            jnp.concatenate([tiles[bit], tiles[3]], axis=1),
        ],
        axis=0,
    )


def unpair_tiles(pairs, bit):
    other = 3 - bit
    tiles = [None] * 4
    tiles[0], tiles[other] = pairs[:WIDTH, :128], pairs[:WIDTH, 128:]
    tiles[bit], tiles[3] = pairs[WIDTH:, :128], pairs[WIDTH:, 128:]
    return tiles


def swap_tiles(tiles):
    split = [quarters(t.astype(F32)) for t in tiles]
    moved = [swap_groups([split[t][q] for t in range(4)]) for q in range(4)]
    return [jnp.concatenate([moved[q][t] for q in range(4)], axis=0).astype(BF16) for t in range(4)]


def main_kernel(
    in_ref, win_ref, wint_ref, wout_ref, woutt_ref, b_ref,
    ret_ref, keep_ref, send_ref,
    n_ref, nhat_ref, inv_ref, h_ref, dv_ref, gp_ref, gy_ref, gb_ref,
):
    def load(at, block):
        tiles = []
        for t in range(4):
            parts = [in_ref[block(t, g), QUARTER * at : QUARTER * (at + 1), :].astype(F32) for g in range(4)]
            tiles.append(jnp.concatenate(swap_groups(parts), axis=0).astype(BF16))
        return tiles

    def store(at, tiles, block):
        for t in range(4):
            for g, part in enumerate(swap_groups(quarters(tiles[t].astype(F32)))):
                ret_ref[block(t, g), QUARTER * at : QUARTER * (at + 1), :] = part.astype(BF16)

    def by_high(t, g):
        return group_of(t >> 1, g >> 1, t & 1, g & 1)

    def by_low(t, g):
        return group_of(g >> 1, t >> 1, g & 1, t & 1)

    bits = (2, 1, 2, 1)
    tiles = load(0, by_high)
    for s in range(4):
        if s == 2:
            tiles = swap_tiles(tiles)
        pairs = pair_tiles(tiles, bits[s])
        values = pairs.astype(F32)
        centered = values - jnp.mean(values, axis=0, keepdims=True)
        inverse = lax.rsqrt(jnp.mean(centered * centered, axis=0, keepdims=True) + 1e-05)
        nhat = centered * inverse
        normed = nhat.astype(BF16)
        n_ref[s] = normed
        nhat_ref[s] = nhat
        inv_ref[s] = jnp.broadcast_to(inverse, (8, CHUNK))
        for j in range(3):
            rows = slice(CHUNK * j, CHUNK * (j + 1))
            bias = b_ref[rows, :]
            pre = jnp.dot(win_ref[rows, :], normed, preferred_element_type=F32)
            pre = pre + jnp.concatenate([bias, bias], axis=1)
            value, deriv = gelu_pair(pre)
            h_ref[s, rows, :] = value.astype(BF16)
            dv_ref[s, rows, :] = deriv
        branch = jnp.dot(woutt_ref[...], h_ref[s], preferred_element_type=F32)
        tiles = unpair_tiles((values + branch).astype(BF16), bits[s])
    store(0, tiles, by_low)

    tiles = load(1, by_low)
    for s in range(3, -1, -1):
        if s == 1:
            tiles = swap_tiles(tiles)
        grad_y = pair_tiles(tiles, bits[s])
        gy_ref[s] = grad_y
        for j in range(3):
            rows = slice(CHUNK * j, CHUNK * (j + 1))
            grad_pre = jnp.dot(wout_ref[rows, :], grad_y, preferred_element_type=F32) * dv_ref[s, rows, :]
            gp_ref[s, rows, :] = grad_pre.astype(BF16)
            folded = grad_pre[:, :128] + grad_pre[:, 128:]
            if s == 3:
                gb_ref[rows, :] = folded
            else:
                gb_ref[rows, :] += folded
        grad_norm = jnp.dot(wint_ref[...], gp_ref[s], preferred_element_type=F32)
        nhat = nhat_ref[s]
        grad_pair = grad_y.astype(F32) + inv_ref[s, 0:1, :] * (
            grad_norm
            - jnp.mean(grad_norm, axis=0, keepdims=True)
            - nhat * jnp.mean(grad_norm * nhat, axis=0, keepdims=True)
        )
        tiles = unpair_tiles(grad_pair.astype(BF16), bits[s])
    store(1, tiles, by_high)

    def over_positions(a, b):
        return lax.dot_general(a, b, (((1,), (1,)), ((), ())), preferred_element_type=F32)

    lane = lax.broadcasted_iota(jnp.int32, (8, PAIR), 1)
    for j in range(4):
        rows = slice(WIDTH * j, WIDTH * (j + 1))
        grad_in = sum(over_positions(gp_ref[s, rows, :], n_ref[s]) for s in range(4))
        grad_out = sum(over_positions(h_ref[s, rows, :], gy_ref[s]) for s in range(4))
        grad_bias = jnp.sum(gb_ref[rows, :], axis=1, keepdims=True)
        for b in range(8):
            at = slice(24 * b, 24 * (b + 1))
            thirds = [grad_bias[24 * b + 8 * k : 24 * b + 8 * (k + 1)] for k in range(3)]
            extra = jnp.where(lane == 0, thirds[0], jnp.where(lane == 1, thirds[1], thirds[2]))
            block = jnp.concatenate([grad_in[at], grad_out[at], extra], axis=0).astype(BF16)
            (keep_ref if j < 2 else send_ref)[8 * (j % 2) + b] = block


def plane_kernel(in_ref, out_ref, total_ref):
    total = in_ref[0].astype(F32)
    for i in range(1, 16):
        total = total + in_ref[i].astype(F32)
    total_ref[0:56, :] = total
    total_ref[56:64, :] = jnp.zeros((8, PAIR), F32)
    for z in range(8):
        out_ref[z] = jnp.concatenate([total_ref[8 * i + z : 8 * i + z + 1, :] for i in range(8)], axis=0)


def call(kernel, out_shapes, scratch=(), smem=0, **args):
    vmem = pl.BlockSpec(memory_space=pltpu.VMEM)
    spec = [pl.BlockSpec(memory_space=pltpu.SMEM)] * smem

    def run(*operands):
        return pl.pallas_call(
            kernel,
            out_shape=out_shapes,
            in_specs=spec + [vmem] * (len(operands) - smem),
            out_specs=jax.tree.map(lambda _: vmem, out_shapes),
            scratch_shapes=scratch,
            compiler_params=pltpu.CompilerParams(vmem_limit_bytes=VMEM_LIMIT),
            **args,
        )(*operands)

    return run


def shape(*dims, dtype=BF16):
    return jax.ShapeDtypeStruct(dims, dtype)


def on_device(inputs, upstream, w_in, w_out, bias):
    rows, width = inputs.shape
    tokens = rows * lax.axis_size(BITS)
    core = lax.axis_index("core").astype(jnp.int32).reshape(1)
    packed = call(pack_kernel, shape(16, 2 * QUARTER, 128))(inputs.T, upstream.T)
    blocks = lax.all_to_all(packed, SECTION_GROUP, 0, 0, tiled=True)
    ordered = call(
        order_kernel,
        (
            shape(HIDDEN, PAIR), shape(PAIR, HIDDEN), shape(HIDDEN, PAIR), shape(PAIR, HIDDEN),
            shape(HIDDEN, 128, dtype=F32),
        ),
        smem=1,
    )(core, w_in, w_out, bias.reshape(1, HIDDEN))
    back, keep, send = call(
        main_kernel,
        (shape(16, 2 * QUARTER, 128), shape(16, 56, PAIR), shape(16, 56, PAIR)),
        scratch=(
            pltpu.VMEM((4, PAIR, CHUNK), BF16),
            pltpu.VMEM((4, PAIR, CHUNK), F32),
            pltpu.VMEM((4, 8, CHUNK), F32),
            pltpu.VMEM((4, HIDDEN, CHUNK), BF16),
            pltpu.VMEM((4, HIDDEN, CHUNK), F32),
            pltpu.VMEM((4, HIDDEN, CHUNK), BF16),
            pltpu.VMEM((4, PAIR, CHUNK), BF16),
            pltpu.VMEM((HIDDEN, 128), F32),
        ),
    )(blocks, *ordered)
    other = lax.ppermute(send, "core", [(0, 1), (1, 0)])
    summed = (keep.astype(F32) + other.astype(F32)).astype(BF16)
    plane = lax.all_to_all(summed, PLANE_GROUP, 0, 0, tiled=True)
    columns = call(plane_kernel, shape(8, 8, PAIR, dtype=F32), scratch=(pltpu.VMEM((64, PAIR), F32),))(plane)
    column = lax.all_to_all(columns, COLUMN_GROUP, 0, 0, tiled=True)
    total = jnp.sum(column, axis=0) * (1.0 / math.sqrt(float(tokens)))
    returned = lax.all_to_all(back, SECTION_GROUP, 0, 0, tiled=True)
    features, grads = call(unpack_kernel, (shape(width, rows), shape(width, rows)))(returned)
    return features.T, grads.T, total[0:3], total[3:6], total[6, 0:3]


def solution(mesh):
    bits = Mesh(mesh.devices.reshape((2,) * len(BITS)), BITS)
    in_specs = (P(BITS, None), P(BITS, None), P(), P(), P())
    out_specs = (P(BITS, None), P(BITS, None), P(BITS, None), P(BITS, None), P(BITS))
    return jax.shard_map(on_device, mesh=bits, in_specs=in_specs, out_specs=out_specs, check_vma=False)
```

time: 435 us -> 95.1 us (0.22)
  waiting for transfers between devices: 291 us -> 30.1 us
  blocking collectives: 77.6 us -> 17.8 us
  matrix products: 26.5 us -> 0 us
  Pallas kernels: 0 us -> 22.4 us
  between operations: 14.5 us -> 0.67 us
  other arithmetic: 9.97 us -> 1.29 us
  starting transfers between devices: 12.5 us -> 19.8 us
    unnamed x2 -> x0, waiting for transfers between devices: 256 us -> none
    unnamed x1 -> x0, blocking collectives: 77.6 us -> none
    ppermute x8 -> x1, waiting for transfers between devices: 35.2 us -> 2.35 us  [on_device(): other = lax.ppermute(send, 'core', [(0, 1), (1, 0)])]
    all_to_all x0 -> x3, waiting for transfers between devices: none -> 27.7 us  [the longest x1 11.9 us: on_device(): returned = lax.all_to_all(back, SECTION_GROUP, 0, 0, tiled=True)]
    dot_general x24 -> x0, matrix products: 26.5 us -> none  [the longest x4 8.03 us: unit_backward(): lax.dot_general(hidden, grad_y, (((0,), (0,)), ((), ())), preferred_eleme...]
    pallas_call x0 -> x5, Pallas kernels: none -> 22.4 us  [run(): pl.pallas_call(kernel, out_shape=out_shapes, in_specs=spec + [vmem] * (le...]
    all_to_all x0 -> x3, starting transfers between devices: none -> 19.8 us  [the longest x1 8.65 us: on_device(): blocks = lax.all_to_all(packed, SECTION_GROUP, 0, 0, tiled=True)]
    all_to_all x0 -> x1, blocking collectives: none -> 17.8 us  [on_device(): plane = lax.all_to_all(summed, PLANE_GROUP, 0, 0, tiled=True)]
  transfers between devices with their start and end apart: 9 -> 4, of which waited for: 8 -> 4; matrix products, arithmetic and copies ran while one was open for 2% -> 1% of each run, Pallas kernels for 0% -> 9%
where the time goes in v1:
time: 95.1 us; the launch traced here: 94.5 us
  waiting for transfers between devices  30.1 us (32%)
  Pallas kernels  22.4 us (24%)
  starting transfers between devices  19.8 us (21%)
  blocking collectives  17.8 us (19%)
  local copies, waits for them, and re-layouts  2.47 us (3%)
  other arithmetic  1.29 us (1%)
    pallas_call x5, Pallas kernels, run(): pl.pallas_call(kernel, out_shape=out_shapes, in_specs=spec + [vmem] * (le...  22.4 us
    all_to_all x1, blocking collectives, on_device(): plane = lax.all_to_all(summed, PLANE_GROUP, 0, 0, tiled=True)  17.8 us
    all_to_all x1, waiting for transfers between devices, on_device(): returned = lax.all_to_all(back, SECTION_GROUP, 0, 0, tiled=True)  11.9 us
    all_to_all x1, waiting for transfers between devices, on_device(): blocks = lax.all_to_all(packed, SECTION_GROUP, 0, 0, tiled=True)  9.41 us
    all_to_all x1, starting transfers between devices, on_device(): blocks = lax.all_to_all(packed, SECTION_GROUP, 0, 0, tiled=True)  8.65 us
    all_to_all x1, waiting for transfers between devices, on_device(): column = lax.all_to_all(columns, COLUMN_GROUP, 0, 0, tiled=True)  6.43 us
    all_to_all x1, starting transfers between devices, on_device(): column = lax.all_to_all(columns, COLUMN_GROUP, 0, 0, tiled=True)  6.32 us
    all_to_all x1, starting transfers between devices, on_device(): returned = lax.all_to_all(back, SECTION_GROUP, 0, 0, tiled=True)  4.8 us
  transfers between devices with their start and end apart: 4, of which 4 were waited for; matrix products, arithmetic and copies ran while one was open for 1% of the time, Pallas kernels for 9%

profile of v1, /device:TPU:2, one launch (start us, length us, event | category | flops | bytes accessed | tf_op | source)
XLA Modules:
  0.0 94.5 jit_solution(15573836903031608897)
XLA Ops:
  0.6 0.0 copy-start.2
  0.6 2.4 %shard_map.92 = bf16[16,96,128]{2,1,0:T(8,128)(2,1)} custom-call(bf16[192,512]{1,0:T(8,128)(2,1)} %bitcast.7, bf16[192,512]{1,0:T(8,128)(2,1)} %bitcast.8), custom_call_target="tpu_custom_call" | custom-call | tf_op jit(solution)/shard_map/pallas_call | solution.py:224
  3.0 8.7 %all-to-all-start = ((bf16[16,96,128]{2,1,0:T(8,128)(2,1)}), bf16[16,96,128]{2,1,0:T(8,128)(2,1)S(1)}, u32[]{:S(2)}, u32[]{:S(2)}) async-start(bf16[16,96,128]{2,1,0:T(8,128)(2,1)} %shard_map.92), calls=%async_computation | async-start | bytes 786432 | tf_op jit(solution)/shard_map/all_to_all | solution.py:246
  11.7 0.0 copy-done.2
  11.7 0.6 reshape.17.bias_ref
  12.3 3.9 %shard_map.93 = (bf16[768,384]{1,0:T(8,128)(2,1)}, bf16[384,768]{1,0:T(8,128)(2,1)}, bf16[768,384]{1,0:T(8,128)(2,1)}, bf16[384,768]{1,0:T(8,128)(2,1)}, f32[768,128]{1,0:T(8,128)}) custom-call(s32[1]{0:T(128)} %bitcast.2.core_ref, bf16[768,384]{1,0:T(8,128)(2,1)} %w_in_ref.1, bf16[768,384]{1,0:T(8,128)(2,1)} %w_out_ref.1, f32[1,768]{1,0:T(1,128)} %reshape.17.bias_ref), custom_call_target="tpu_custom_call" | custom-call | tf_op jit(solution)/shard_map/pallas_call | solution.py:224
  16.2 9.4 %all-to-all-done.in_ref = bf16[16,96,128]{2,1,0:T(8,128)(2,1)S(1)} async-done(((bf16[16,96,128]{2,1,0:T(8,128)(2,1)}), bf16[16,96,128]{2,1,0:T(8,128)(2,1)S(1)}, u32[]{:S(2)}, u32[]{:S(2)}) %all-to-all-start) | async-done | bytes 393248 | tf_op jit(solution)/shard_map/all_to_all | solution.py:246
  25.6 0.0 copy-start
  25.6 0.8 copy-done
  26.4 12.0 %shard_map.94 = (bf16[16,96,128]{2,1,0:T(8,128)(2,1)}, bf16[16,56,384]{2,1,0:T(8,128)(2,1)}, bf16[16,56,384]{2,1,0:T(8,128)(2,1)}) custom-call(bf16[16,96,128]{2,1,0:T(8,128)(2,1)} %copy-done, bf16[768,384]{1,0:T(8,128)(2,1)} %get-tuple-element.15.win_ref, bf16[384,768]{1,0:T(8,128)(2,1)} %get-tuple-element.16.wint_ref, ...), custom_call_target="tpu_custom_call" | custom-call | tf_op jit(solution)/shard_map/pallas_call | solution.py:224
  38.3 0.0 collective-permute-start
  38.3 2.4 %collective-permute-done = bf16[16,56,384]{2,1,0:T(8,128)(2,1)S(1)} collective-permute-done((bf16[16,56,384]{2,1,0:T(8,128)(2,1)}, bf16[16,56,384]{2,1,0:T(8,128)(2,1)S(1)}, u32[]{:S(2)}, u32[]{:S(2)}) %collective-permute-start) | collective-permute-done | bytes 688160 | tf_op jit(solution)/shard_map/ppermute | solution.py:269
  40.7 1.3 %add_convert_fusion = bf16[16,56,384]{2,1,0:T(8,128)(2,1)S(1)} fusion(bf16[16,56,384]{2,1,0:T(8,128)(2,1)S(1)} %collective-permute-done, bf16[16,56,384]{2,1,0:T(8,128)(2,1)} %get-tuple-element.23), kind=kLoop, calls=%fused_computation | loop fusion | flops 1376256 | bytes 2064384 | tf_op jit(solution)/shard_map/convert_element_type | solution.py:270
  42.0 17.8 %all_to_all.20.in_ref = bf16[16,56,384]{2,1,0:T(8,128)(2,1)} all-to-all(bf16[16,56,384]{2,1,0:T(8,128)(2,1)S(1)} %add_convert_fusion), channel_id=1, replica_groups=mesh['y1'=2,'y0'=2,'zh'=2,'core'=2,'zl1'=2,'zl0'=2,'x1'=2,'x0'=2] {'y1',..., dimensions={0} | all-to-all | bytes 1376256 | tf_op jit(solution)/shard_map/all_to_all | solution.py:271
  59.8 4.8 %all-to-all-start.1 = ((bf16[16,96,128]{2,1,0:T(8,128)(2,1)}), bf16[16,96,128]{2,1,0:T(8,128)(2,1)S(1)}, u32[]{:S(2)}, u32[]{:S(2)}) async-start(bf16[16,96,128]{2,1,0:T(8,128)(2,1)} %get-tuple-element.20), calls=%async_computation.1 | async-start | bytes 786432 | tf_op jit(solution)/shard_map/all_to_all | solution.py:275
  64.6 1.9 %shard_map.96 = f32[8,8,384]{2,1,0:T(8,128)} custom-call(bf16[16,56,384]{2,1,0:T(8,128)(2,1)} %all_to_all.20.in_ref), custom_call_target="tpu_custom_call" | custom-call | tf_op jit(solution)/shard_map/pallas_call | solution.py:224
  66.4 11.9 %all-to-all-done.1.in_ref = bf16[16,96,128]{2,1,0:T(8,128)(2,1)S(1)} async-done(((bf16[16,96,128]{2,1,0:T(8,128)(2,1)}), bf16[16,96,128]{2,1,0:T(8,128)(2,1)S(1)}, u32[]{:S(2)}, u32[]{:S(2)}) %all-to-all-start.1) | async-done | bytes 393248 | tf_op jit(solution)/shard_map/all_to_all | solution.py:275
  78.3 0.0 copy-start.1
  78.3 6.3 %all-to-all-start.3 = ((f32[8,8,384]{2,1,0:T(8,128)}), f32[8,8,384]{2,1,0:T(8,128)S(1)}, u32[]{:S(2)}, u32[]{:S(2)}) async-start(f32[8,8,384]{2,1,0:T(8,128)} %shard_map.96), calls=%async_computation.3 | async-start | bytes 196608 | tf_op jit(solution)/shard_map/all_to_all | solution.py:273
  84.7 0.0 copy-done.1
  84.7 2.3 %shard_map.95 = (bf16[192,512]{1,0:T(8,128)(2,1)}, bf16[192,512]{1,0:T(8,128)(2,1)}) custom-call(bf16[16,96,128]{2,1,0:T(8,128)(2,1)} %copy-done.1), custom_call_target="tpu_custom_call" | custom-call | tf_op jit(solution)/shard_map/pallas_call | solution.py:224
  87.0 6.4 %all-to-all-done.3 = f32[8,8,384]{2,1,0:T(8,128)S(1)} async-done(((f32[8,8,384]{2,1,0:T(8,128)}), f32[8,8,384]{2,1,0:T(8,128)S(1)}, u32[]{:S(2)}, u32[]{:S(2)}) %all-to-all-start.3) | async-done | bytes 98336 | tf_op jit(solution)/shard_map/all_to_all | solution.py:273
  93.4 0.5 slice_bitcast_fusion
  93.9 0.6 fusion
  (2 shorter events, 0.0 us)
Async XLA Ops:
  0.6 11.1 %copy-start.2 = (f32[768]{0:T(1024)S(1)}, f32[768]{0:T(1024)}, u32[]{:S(2)}) copy-start(f32[768]{0:T(1024)} %param.9) | copy-start | bytes 9220
  3.0 22.6 %all-to-all-start = ((bf16[16,96,128]{2,1,0:T(8,128)(2,1)}), bf16[16,96,128]{2,1,0:T(8,128)(2,1)S(1)}, u32[]{:S(2)}, u32[]{:S(2)}) async-start(bf16[16,96,128]{2,1,0:T(8,128)(2,1)} %shard_map.92), calls=%async_computation | async-start | bytes 786432 | tf_op jit(solution)/shard_map/all_to_all | solution.py:246
  25.6 0.8 copy-start
  38.3 2.4 %collective-permute-start = (bf16[16,56,384]{2,1,0:T(8,128)(2,1)}, bf16[16,56,384]{2,1,0:T(8,128)(2,1)S(1)}, u32[]{:S(2)}, u32[]{:S(2)}) collective-permute-start(bf16[16,56,384]{2,1,0:T(8,128)(2,1)} %get-tuple-element.24), channel_id=1, source_target_pairs={{0,16},{16,0},{1,17},{17,1},{2,18},{18,2},{3,19},{19,3},{4,20},{20... | collective-permute-start | bytes 2064392 | tf_op jit(solution)/shard_map/ppermute | solution.py:269
  59.8 18.5 %all-to-all-start.1 = ((bf16[16,96,128]{2,1,0:T(8,128)(2,1)}), bf16[16,96,128]{2,1,0:T(8,128)(2,1)S(1)}, u32[]{:S(2)}, u32[]{:S(2)}) async-start(bf16[16,96,128]{2,1,0:T(8,128)(2,1)} %get-tuple-element.20), calls=%async_computation.1 | async-start | bytes 786432 | tf_op jit(solution)/shard_map/all_to_all | solution.py:275
  78.3 6.3 %copy-start.1 = (bf16[16,96,128]{2,1,0:T(8,128)(2,1)}, bf16[16,96,128]{2,1,0:T(8,128)(2,1)S(1)}, u32[]{:S(2)}) copy-start(bf16[16,96,128]{2,1,0:T(8,128)(2,1)S(1)} %all-to-all-done.1.in_ref) | copy-start | bytes 1179652
  78.3 15.1 %all-to-all-start.3 = ((f32[8,8,384]{2,1,0:T(8,128)}), f32[8,8,384]{2,1,0:T(8,128)S(1)}, u32[]{:S(2)}, u32[]{:S(2)}) async-start(f32[8,8,384]{2,1,0:T(8,128)} %shard_map.96), calls=%async_computation.3 | async-start | bytes 196608 | tf_op jit(solution)/shard_map/all_to_all | solution.py:273

commit v2 on v1

v2 whole, which is shorter than its diff:
```python
import functools
import math

import jax
import jax.numpy as jnp
from jax import lax
from jax.experimental import pallas as pl
from jax.experimental.pallas import tpu as pltpu
from jax.sharding import Mesh
from jax.sharding import PartitionSpec as P

BITS = ("y1", "y0", "zh", "core", "zl1", "zl0", "x1", "x0")
SECTION_GROUP = ("y1", "core", "zl1", "x0")
PLANE_GROUP = ("y1", "y0", "x1", "x0")
COLUMN_GROUP = ("zh", "zl1", "zl0")
HIDDEN, WIDTH, PAIR = 768, 192, 384
OUT_AT = PAIR + 128
WIDE = PAIR + 16
QUARTER = 48
BLOCK = 152
CHUNK = 256
BF16, F32 = jnp.bfloat16, jnp.float32
MIB = 1024 * 1024


def swap_groups(parts):
    lane = lax.broadcasted_iota(jnp.int32, parts[0].shape, 1)
    for stride, at in ((2, 64), (1, 32)):
        low = (lane & at) == 0
        out = list(parts)
        for i in range(4):
            if not i & stride:
                a, b = parts[i], parts[i | stride]
                out[i] = jnp.where(low, a, pltpu.roll(b, at, 1))
                out[i | stride] = jnp.where(low, pltpu.roll(a, 128 - at, 1), b)
        parts = out
    return parts


def quarters(tile):
    return [tile[QUARTER * q : QUARTER * (q + 1)] for q in range(4)]


def group_of(y1, core, zl1, x0):
    return 8 * y1 + 4 * core + 2 * zl1 + x0


def pack_kernel(x_hbm, g_hbm, out_ref, x_ref, g_ref, sems):
    copies = [
        pltpu.make_async_copy(x_hbm, x_ref, sems.at[0]),
        pltpu.make_async_copy(g_hbm, g_ref, sems.at[1]),
    ]
    for copy in copies:
        copy.start()
    for at, ref in enumerate((x_ref, g_ref)):
        copies[at].wait()
        for t in range(4):
            tile = ref[:, 128 * t : 128 * (t + 1)].astype(F32)
            for g, part in enumerate(swap_groups(quarters(tile))):
                out_ref[4 * t + g, QUARTER * at : QUARTER * (at + 1), :] = part.astype(BF16)


def unpack_kernel(me_ref, in_ref, f_ref, g_ref):
    me = me_ref[0]
    for at, ref in enumerate((f_ref, g_ref)):
        for t in range(4):
            parts = [
                in_ref[me ^ (4 * t + g), QUARTER * at : QUARTER * (at + 1), :].astype(F32) for g in range(4)
            ]
            for q, part in enumerate(swap_groups(parts)):
                ref[QUARTER * q : QUARTER * (q + 1), 128 * t : 128 * (t + 1)] = part.astype(BF16)


def order_kernel(core_ref, w_in_ref, w_out_ref, bias_ref, w_ref, wt_ref):
    core = core_ref[0]

    def place(unit):
        device = (unit * 21846) >> 16
        third = unit - 3 * device
        block = (device >> 6) * 4 + (device & 3)
        z = ((device >> 5) & 1) * 4 + ((device >> 2) & 3)
        return (((device >> 4) & 1) ^ core) * (HIDDEN // 2) + block * 24 + third * 8 + z

    shape = (HIDDEN, HIDDEN)
    hit = lax.broadcasted_iota(jnp.int32, shape, 0) == place(lax.broadcasted_iota(jnp.int32, shape, 1))
    pick = hit.astype(F32).astype(BF16)
    for i, (ref, at) in enumerate(((w_in_ref, 0), (w_out_ref, OUT_AT))):
        moved = jnp.dot(pick, ref[...], preferred_element_type=F32)
        w_ref[:, at : at + PAIR] = moved.astype(BF16)
        wt_ref[PAIR * i : PAIR * (i + 1), :] = moved.T.astype(BF16)
    bias = jnp.sum(jnp.where(hit, bias_ref[...], 0.0), axis=1, keepdims=True)
    lane = lax.broadcasted_iota(jnp.int32, (HIDDEN, 128), 1)
    columns = jnp.zeros((HIDDEN, 128), F32)
    for i in range(3):
        piece = bias.astype(BF16).astype(F32)
        columns = jnp.where(lane == i, piece, columns)
        bias = bias - piece
    w_ref[:, PAIR : PAIR + 128] = columns.astype(BF16)


def gelu_pair(pre):
    coeff = math.sqrt(2.0 / math.pi)
    square = pre * pre
    tangent = jnp.tanh(coeff * pre * (1.0 + 0.044715 * square))
    half = 0.5 * (1.0 + tangent)
    value = pre * half
    deriv = half + 0.5 * coeff * pre * (1.0 - tangent * tangent) * (1.0 + 3.0 * 0.044715 * square)
    return value, deriv


def pair_tiles(tiles, bit):
    other = 3 - bit
    return jnp.concatenate(
        [
            jnp.concatenate([tiles[0], tiles[other]], axis=1),
            jnp.concatenate([tiles[bit], tiles[3]], axis=1),
        ],
        axis=0,
    )


def unpair_tiles(pairs, bit):
    other = 3 - bit
    tiles = [None] * 4
    tiles[0], tiles[other] = pairs[:WIDTH, :128], pairs[:WIDTH, 128:]
    tiles[bit], tiles[3] = pairs[WIDTH:, :128], pairs[WIDTH:, 128:]
    return tiles


def swap_tiles(tiles):
    split = [quarters(t.astype(F32)) for t in tiles]
    moved = [swap_groups([split[t][q] for t in range(4)]) for q in range(4)]
    return [jnp.concatenate([moved[q][t] for q in range(4)], axis=0).astype(BF16) for t in range(4)]


def main_kernel(
    me_ref, in_ref, w_ref, wt_ref,
    ret_ref, keep_ref, send_ref,
    n_ref, nhat_ref, inv_ref, h_ref, dv_ref, gp_ref, gy_ref,
):
    me = me_ref[0]

    def load(at, block):
        tiles = []
        for t in range(4):
            parts = [in_ref[block(t, g), QUARTER * at : QUARTER * (at + 1), :].astype(F32) for g in range(4)]
            tiles.append(jnp.concatenate(swap_groups(parts), axis=0).astype(BF16))
        return tiles

    def store(at, tiles, block):
        for t in range(4):
            for g, part in enumerate(swap_groups(quarters(tiles[t].astype(F32)))):
                ret_ref[me ^ block(t, g), QUARTER * at : QUARTER * (at + 1), :] = part.astype(BF16)

    def by_high(t, g):
        return group_of(t >> 1, g >> 1, t & 1, g & 1)

    def by_low(t, g):
        return group_of(g >> 1, t >> 1, g & 1, t & 1)

    bits = (2, 1, 2, 1)
    ones = (lax.broadcasted_iota(jnp.int32, (WIDE - PAIR, CHUNK), 0) < 3).astype(F32)
    tiles = load(0, by_high)
    for s in range(4):
        if s == 2:
            tiles = swap_tiles(tiles)
        pairs = pair_tiles(tiles, bits[s])
        values = pairs.astype(F32)
        centered = values - jnp.mean(values, axis=0, keepdims=True)
        inverse = lax.rsqrt(jnp.mean(centered * centered, axis=0, keepdims=True) + 1e-05)
        nhat = centered * inverse
        normed = jnp.concatenate([nhat, ones], axis=0).astype(BF16)
        n_ref[s] = normed
        nhat_ref[s] = nhat
        inv_ref[s] = jnp.broadcast_to(inverse, (8, CHUNK))
        for j in range(3):
            rows = slice(CHUNK * j, CHUNK * (j + 1))
            pre = jnp.dot(w_ref[rows, :WIDE], normed, preferred_element_type=F32)
            value, deriv = gelu_pair(pre)
            h_ref[s, rows, :] = value.astype(BF16)
            dv_ref[s, rows, :] = deriv
        branch = jnp.dot(wt_ref[PAIR:, :], h_ref[s], preferred_element_type=F32)
        tiles = unpair_tiles((values + branch).astype(BF16), bits[s])
    store(0, tiles, by_low)

    tiles = load(1, by_low)
    for s in range(3, -1, -1):
        if s == 1:
            tiles = swap_tiles(tiles)
        grad_y = pair_tiles(tiles, bits[s])
        gy_ref[s] = grad_y
        for j in range(3):
            rows = slice(CHUNK * j, CHUNK * (j + 1))
            grad_pre = jnp.dot(w_ref[rows, OUT_AT:], grad_y, preferred_element_type=F32) * dv_ref[s, rows, :]
            gp_ref[s, rows, :] = grad_pre.astype(BF16)
        grad_norm = jnp.dot(wt_ref[:PAIR, :], gp_ref[s], preferred_element_type=F32)
        nhat = nhat_ref[s]
        grad_pair = grad_y.astype(F32) + inv_ref[s, 0:1, :] * (
            grad_norm
            - jnp.mean(grad_norm, axis=0, keepdims=True)
            - nhat * jnp.mean(grad_norm * nhat, axis=0, keepdims=True)
        )
        tiles = unpair_tiles(grad_pair.astype(BF16), bits[s])
    store(1, tiles, by_high)

    def over_positions(a, b):
        return lax.dot_general(a, b, (((1,), (1,)), ((), ())), preferred_element_type=F32)

    lane = lax.broadcasted_iota(jnp.int32, (8, 128), 1)
    for j in range(4):
        rows = slice(WIDTH * j, WIDTH * (j + 1))
        grad_in = sum(over_positions(gp_ref[s, rows, :], n_ref[s]) for s in range(4))
        grad_out = sum(over_positions(h_ref[s, rows, :], gy_ref[s]) for s in range(4))
        for b in range(8):
            at = slice(24 * b, 24 * (b + 1))
            tiles = [g[at, 128 * i : 128 * (i + 1)] for g in (grad_in, grad_out) for i in range(3)]
            thirds = [grad_in[24 * b + 8 * k : 24 * b + 8 * (k + 1), PAIR : PAIR + 1] for k in range(3)]
            extra = jnp.where(lane == 0, thirds[0], jnp.where(lane == 1, thirds[1], thirds[2]))
            (keep_ref if j < 2 else send_ref)[8 * (j % 2) + b] = jnp.concatenate(tiles + [extra], axis=0).astype(BF16)


def plane_kernel(in_ref, out_ref, total_ref):
    total = in_ref[0].astype(F32)
    for i in range(1, 16):
        total = total + in_ref[i].astype(F32)
    total_ref[...] = total
    for z in range(8):
        rows = [total_ref[pl.ds(z, 19, stride=8), :], jnp.zeros((5, 128), F32)]
        out_ref[z] = jnp.concatenate(rows, axis=0).astype(BF16)


def column_kernel(factor, in_ref, w_in_ref, w_out_ref, bias_ref):
    total = in_ref[0].astype(F32)
    for i in range(1, 8):
        total = total + in_ref[i].astype(F32)
    total = total * factor
    for i in range(3):
        w_in_ref[:, 128 * i : 128 * (i + 1)] = total[3 * i : 3 * i + 3]
        w_out_ref[:, 128 * i : 128 * (i + 1)] = total[9 + 3 * i : 12 + 3 * i]
    bias_ref[...] = total[18:19, 0:3]


def call(kernel, out_shapes, scratch=(), smem=0, vmem_mib=4, space=None):
    vmem = pl.BlockSpec(memory_space=pltpu.VMEM)
    spec = [pl.BlockSpec(memory_space=pltpu.SMEM)] * smem

    def run(*operands):
        return pl.pallas_call(
            kernel,
            out_shape=out_shapes,
            in_specs=spec + [space or vmem] * (len(operands) - smem),
            out_specs=jax.tree.map(lambda _: vmem, out_shapes),
            scratch_shapes=scratch,
            compiler_params=pltpu.CompilerParams(vmem_limit_bytes=vmem_mib * MIB),
        )(*operands)

    return run


def shape(*dims, dtype=BF16):
    return jax.ShapeDtypeStruct(dims, dtype)


def give_back(blocks):
    held = blocks.reshape((2, 2, 2, 2) + blocks.shape[1:])
    for axis, at in (("core", 1), ("x0", 3), ("zl1", 2), ("y1", 0)):
        stay = lax.index_in_dim(held, 0, at, keepdims=True)
        leave = lax.index_in_dim(held, 1, at, keepdims=True)
        held = jnp.concatenate([stay, swap(leave, axis)], axis=at)
    return held.reshape(blocks.shape)


def swap(block, axis):
    return lax.ppermute(block, axis, [(0, 1), (1, 0)])


def on_device(inputs, upstream, w_in, w_out, bias):
    rows, width = inputs.shape
    tokens = rows * lax.axis_size(BITS)
    core = lax.axis_index("core").astype(jnp.int32).reshape(1)
    me = sum(lax.axis_index(a).astype(jnp.int32) << (3 - i) for i, a in enumerate(SECTION_GROUP)).reshape(1)
    hbm = pl.BlockSpec(memory_space=pltpu.HBM)
    landing = pltpu.VMEM((width, rows), BF16)
    packed = call(
        pack_kernel, shape(16, 2 * QUARTER, 128), scratch=(landing, landing, pltpu.SemaphoreType.DMA((2,))), space=hbm, vmem_mib=60
    )(inputs.T, upstream.T)
    blocks = lax.all_to_all(packed, SECTION_GROUP, 0, 0, tiled=True)
    ordered = call(order_kernel, (shape(HIDDEN, OUT_AT + PAIR), shape(2 * PAIR, HIDDEN)), smem=1, vmem_mib=12)(
        core, w_in, w_out, bias.reshape(1, HIDDEN)
    )
    back, keep, send = call(
        main_kernel,
        (shape(16, 2 * QUARTER, 128), shape(16, BLOCK, 128), shape(16, BLOCK, 128)),
        scratch=(
            pltpu.VMEM((4, WIDE, CHUNK), BF16),
            pltpu.VMEM((4, PAIR, CHUNK), F32),
            pltpu.VMEM((4, 8, CHUNK), F32),
            pltpu.VMEM((4, HIDDEN, CHUNK), BF16),
            pltpu.VMEM((4, HIDDEN, CHUNK), F32),
            pltpu.VMEM((4, HIDDEN, CHUNK), BF16),
            pltpu.VMEM((4, PAIR, CHUNK), BF16),
        ),
        smem=1,
        vmem_mib=24,
    )(me, blocks, *ordered)
    other = swap(send, "core")
    summed = (keep.astype(F32) + other.astype(F32)).astype(BF16)
    plane = lax.all_to_all(summed, PLANE_GROUP, 0, 0, tiled=True)
    columns = call(plane_kernel, shape(8, 24, 128), scratch=(pltpu.VMEM((BLOCK, 128), F32),))(plane)
    column = lax.all_to_all(columns, COLUMN_GROUP, 0, 0, tiled=True)
    share_in, share_out, share_bias = call(
        functools.partial(column_kernel, 1.0 / math.sqrt(float(tokens))),
        (shape(3, PAIR, dtype=F32), shape(3, PAIR, dtype=F32), shape(1, 3, dtype=F32)),
    )(column)
    features, grads = call(unpack_kernel, (shape(width, rows), shape(width, rows)), smem=1)(me, give_back(back))
    return features.T, grads.T, share_in, share_out, share_bias.reshape(3)


def solution(mesh):
    bits = Mesh(mesh.devices.reshape((2,) * len(BITS)), BITS)
    in_specs = (P(BITS, None), P(BITS, None), P(), P(), P())
    out_specs = (P(BITS, None), P(BITS, None), P(BITS, None), P(BITS, None), P(BITS))
    return jax.shard_map(on_device, mesh=bits, in_specs=in_specs, out_specs=out_specs, check_vma=False)
```

time: 95.1 us -> 74.3 us (0.78)
  blocking collectives: 17.8 us -> 0 us
  Pallas kernels: 22.4 us -> 15.8 us
  starting transfers between devices: 19.8 us -> 25 us
  local copies, waits for them, and re-layouts: 2.47 us -> 1.1 us
    all_to_all x1 -> x0, blocking collectives: 17.8 us -> none  [on_device(): plane = lax.all_to_all(summed, PLANE_GROUP, 0, 0, tiled=True)]
    all_to_all x1, waiting for transfers between devices: 11.9 us -> 0.01 us  [on_device(): plane = lax.all_to_all(summed, PLANE_GROUP, 0, 0, tiled=True)]
    ppermute x1 -> x5, waiting for transfers between devices: 2.35 us -> 12 us  [swap(): return lax.ppermute(block, axis, [(0, 1), (1, 0)])]
    pallas_call x5 -> x6, Pallas kernels: 22.4 us -> 15.8 us  [run(): pl.pallas_call(kernel, out_shape=out_shapes, in_specs=spec + [space or vm...]
    ppermute x1 -> x5, starting transfers between devices: 0.01 us -> 4.74 us  [swap(): return lax.ppermute(block, axis, [(0, 1), (1, 0)])]
    all_to_all x1, waiting for transfers between devices: 9.41 us -> 11.2 us  [on_device(): blocks = lax.all_to_all(packed, SECTION_GROUP, 0, 0, tiled=True)]
  transfers between devices with their start and end apart: 4 -> 8, of which waited for: 4 -> 4; matrix products, arithmetic and copies ran while one was open for 1% -> 2% of each run, Pallas kernels for 9% -> 5%
where the time goes in v2:
time: 74.3 us; the launch traced here: 73.9 us
  waiting for transfers between devices  30 us (40%)
  starting transfers between devices  25 us (34%)
  Pallas kernels  15.8 us (21%)
  other arithmetic  1.15 us (2%)
  local copies, waits for them, and re-layouts  1.1 us (1%)
  between operations  0.77 us (1%)
    pallas_call x6, Pallas kernels, run(): pl.pallas_call(kernel, out_shape=out_shapes, in_specs=spec + [space or vm...  15.8 us
    ppermute x5, waiting for transfers between devices, swap(): return lax.ppermute(block, axis, [(0, 1), (1, 0)])  12 us
    all_to_all x1, waiting for transfers between devices, on_device(): blocks = lax.all_to_all(packed, SECTION_GROUP, 0, 0, tiled=True)  11.2 us
    all_to_all x1, starting transfers between devices, on_device(): blocks = lax.all_to_all(packed, SECTION_GROUP, 0, 0, tiled=True)  8.66 us
    all_to_all x1, waiting for transfers between devices, on_device(): column = lax.all_to_all(columns, COLUMN_GROUP, 0, 0, tiled=True)  6.84 us
    all_to_all x1, starting transfers between devices, on_device(): column = lax.all_to_all(columns, COLUMN_GROUP, 0, 0, tiled=True)  6.22 us
    all_to_all x1, starting transfers between devices, on_device(): plane = lax.all_to_all(summed, PLANE_GROUP, 0, 0, tiled=True)  5.42 us
    ppermute x5, starting transfers between devices, swap(): return lax.ppermute(block, axis, [(0, 1), (1, 0)])  4.74 us
  transfers between devices with their start and end apart: 8, of which 4 were waited for; matrix products, arithmetic and copies ran while one was open for 2% of the time, Pallas kernels for 5%

profile of v2, /device:TPU:2, one launch (start us, length us, event | category | flops | bytes accessed | tf_op | source)
XLA Modules:
  0.0 73.9 jit_solution(3081303734956245836)
XLA Ops:
  0.6 0.0 copy-start.2
  0.6 0.0 copy-start
  0.7 2.3 %shard_map.92 = bf16[16,96,128]{2,1,0:T(8,128)(2,1)} custom-call(bf16[192,512]{1,0:T(8,128)(2,1)} %bitcast.11, bf16[192,512]{1,0:T(8,128)(2,1)} %bitcast.12), custom_call_target="tpu_custom_call" | custom-call | tf_op jit(solution)/shard_map/pallas_call | solution.py:248
  2.9 8.7 %all-to-all-start = ((bf16[16,96,128]{2,1,0:T(8,128)(2,1)}), bf16[16,96,128]{2,1,0:T(8,128)(2,1)S(1)}, u32[]{:S(2)}, u32[]{:S(2)}) async-start(bf16[16,96,128]{2,1,0:T(8,128)(2,1)} %shard_map.92), calls=%async_computation | async-start | bytes 786432 | tf_op jit(solution)/shard_map/all_to_all | solution.py:287
  11.6 0.0 copy-done.2
  11.6 0.0 copy-done
  11.6 0.0 copy-start.1
  11.7 1.1 %copy-done.1 = bf16[768,384]{1,0:T(8,128)(2,1)S(1)} copy-done((bf16[768,384]{1,0:T(8,128)(2,1)S(1)}, bf16[768,384]{1,0:T(8,128)(2,1)}, u32[]{:S(2)}) %copy-start.1) | copy-done | bytes 589848
  12.7 1.6 %shard_map.93 = (bf16[768,896]{1,0:T(8,128)(2,1)S(1)}, bf16[768,768]{1,0:T(8,128)(2,1)S(1)}) custom-call(s32[1]{0:T(128)} %bitcast.3.core_ref, bf16[768,384]{1,0:T(8,128)(2,1)S(1)} %copy-done, bf16[768,384]{1,0:T(8,128)(2,1)S(1)} %copy-done.1, f32[1,768]{1,0:T(1,128)S(1)} %reshape.30.bias_ref), custom_call_target="tpu_custom_call" | custom-call | tf_op jit(solution)/shard_map/pallas_call | solution.py:248
  14.3 11.2 %all-to-all-done.in_ref = bf16[16,96,128]{2,1,0:T(8,128)(2,1)S(1)} async-done(((bf16[16,96,128]{2,1,0:T(8,128)(2,1)}), bf16[16,96,128]{2,1,0:T(8,128)(2,1)S(1)}, u32[]{:S(2)}, u32[]{:S(2)}) %all-to-all-start) | async-done | bytes 393248 | tf_op jit(solution)/shard_map/all_to_all | solution.py:287
  25.5 9.3 %shard_map.94 = (bf16[16,96,128]{2,1,0:T(8,128)(2,1)S(1)}, bf16[16,152,128]{2,1,0:T(8,128)(2,1)S(1)}, bf16[16,152,128]{2,1,0:T(8,128)(2,1)S(1)}) custom-call(s32[1]{0:T(128)} %bitcast.me_ref, bf16[16,96,128]{2,1,0:T(8,128)(2,1)S(1)} %all-to-all-done.in_ref, bf16[768,896]{1,0:T(8,128)(2,1)S(1)} %get-tuple-element.15.w_ref, ...), custom_call_target="tpu_custom_call" | custom-call | tf_op jit(solution)/shard_map/pallas_call | solution.py:248
  34.8 0.1 collective-permute-start.4
  35.0 0.6 collective-permute-start
  35.5 1.7 %collective-permute-done = bf16[2,1,2,2,96,128]{5,4,3,2,1,0:T(8,128)(2,1)S(1)} collective-permute-done((bf16[2,1,2,2,96,128]{5,4,3,2,1,0:T(8,128)(2,1)S(1)}, bf16[2,1,2,2,96,128]{5,4,3,2,1,0:T(8,128)(2,1)S(1)}, u32[]{:S(2)}, u32[]{:S(2)}) %collective-permute-start) | collective-permute-done | bytes 196640 | tf_op jit(solution)/shard_map/ppermute | solution.py:274
  37.3 0.9 %collective-permute-start.1 = (bf16[2,2,2,1,96,128]{5,4,3,2,1,0:T(8,128)(2,1)S(1)}, bf16[2,2,2,1,96,128]{5,4,3,2,1,0:T(8,128)(2,1)S(1)}, u32[]{:S(2)}, u32[]{:S(2)}) collective-permute-start(bf16[2,2,2,1,96,128]{5,4,3,2,1,0:T(8,128)(2,1)S(1)} %get-tuple-element.30), channel_id=1, source_target_pairs={{0,1},{1,0},{2,3},{3,2},{4,5},{5,4},{6,7},{7,6},{8,9},{9,8},{10,11... | collective-permute-start | bytes 589832 | tf_op jit(solution)/shard_map/ppermute | solution.py:274
  38.2 0.0 collective-permute-done.4
  38.2 1.0 %add_convert_fusion = bf16[16,152,128]{2,1,0:T(8,128)(2,1)} fusion(bf16[16,152,128]{2,1,0:T(8,128)(2,1)S(1)} %collective-permute-done.4, bf16[16,152,128]{2,1,0:T(8,128)(2,1)S(1)} %get-tuple-element.20), kind=kLoop, calls=%fused_computation | loop fusion | flops 1245184 | bytes 1867776 | tf_op jit(solution)/shard_map/convert_element_type | solution.py:307
  39.2 5.4 %all-to-all-start.1 = ((bf16[16,152,128]{2,1,0:T(8,128)(2,1)}), bf16[16,152,128]{2,1,0:T(8,128)(2,1)S(1)}, u32[]{:S(2)}, u32[]{:S(2)}) async-start(bf16[16,152,128]{2,1,0:T(8,128)(2,1)} %add_convert_fusion), calls=%async_computation.1 | async-start | bytes 1245184 | tf_op jit(solution)/shard_map/all_to_all | solution.py:308
  44.6 0.0 collective-permute-done.1
  44.7 0.1 collective-permute-start.2
  44.8 10.3 %collective-permute-done.2 = bf16[2,2,1,2,96,128]{5,4,3,2,1,0:T(8,128)(2,1)S(1)} collective-permute-done((bf16[2,2,1,2,96,128]{5,4,3,2,1,0:T(8,128)(2,1)S(1)}, bf16[2,2,1,2,96,128]{5,4,3,2,1,0:T(8,128)(2,1)S(1)}, u32[]{:S(2)}, u32[]{:S(2)}) %collective-permute-start.2) | collective-permute-done | bytes 196640 | tf_op jit(solution)/shard_map/ppermute | solution.py:274
  55.1 3.1 %collective-permute-start.3 = (bf16[1,2,2,2,96,128]{5,4,3,2,1,0:T(8,128)(2,1)S(1)}, bf16[1,2,2,2,96,128]{5,4,3,2,1,0:T(8,128)(2,1)S(1)}, u32[]{:S(2)}, u32[]{:S(2)}) collective-permute-start(bf16[1,2,2,2,96,128]{5,4,3,2,1,0:T(8,128)(2,1)S(1)} %get-tuple-element.26), channel_id=1, source_target_pairs={{0,128},{128,0},{1,129},{129,1},{2,130},{130,2},{3,131},{131,3},{4... | collective-permute-start | bytes 589832 | tf_op jit(solution)/shard_map/ppermute | solution.py:274
  58.2 0.0 all-to-all-done.1.in_ref
  58.2 0.7 shard_map.96
  58.9 6.2 %all-to-all-start.2 = ((bf16[8,24,128]{2,1,0:T(8,128)(2,1)}), bf16[8,24,128]{2,1,0:T(8,128)(2,1)S(1)}, u32[]{:S(2)}, u32[]{:S(2)}) async-start(bf16[8,24,128]{2,1,0:T(8,128)(2,1)} %shard_map.96), calls=%async_computation.2 | async-start | bytes 98304 | tf_op jit(solution)/shard_map/all_to_all | solution.py:310
  65.1 0.0 collective-permute-done.3
  65.2 1.3 %shard_map.95 = (bf16[192,512]{1,0:T(8,128)(2,1)}, bf16[192,512]{1,0:T(8,128)(2,1)}) custom-call(s32[1]{0:T(128)} %bitcast.me_ref, bf16[16,96,128]{2,1,0:T(8,128)(2,1)S(1)} %bitcast.9), custom_call_target="tpu_custom_call" | custom-call | tf_op jit(solution)/shard_map/pallas_call | solution.py:248
  66.5 6.8 %all-to-all-done.2.in_ref = bf16[8,24,128]{2,1,0:T(8,128)(2,1)S(1)} async-done(((bf16[8,24,128]{2,1,0:T(8,128)(2,1)}), bf16[8,24,128]{2,1,0:T(8,128)(2,1)S(1)}, u32[]{:S(2)}, u32[]{:S(2)}) %all-to-all-start.2) | async-done | bytes 49184 | tf_op jit(solution)/shard_map/all_to_all | solution.py:310
  73.3 0.6 shard_map.97
  (6 shorter events, 0.2 us)
Async XLA Ops:
  0.6 11.0 %copy-start.2 = (f32[768]{0:T(1024)S(1)}, f32[768]{0:T(1024)}, u32[]{:S(2)}) copy-start(f32[768]{0:T(1024)} %param.9) | copy-start | bytes 9220
  0.6 11.0 %copy-start = (bf16[768,384]{1,0:T(8,128)(2,1)S(1)}, bf16[768,384]{1,0:T(8,128)(2,1)}, u32[]{:S(2)}) copy-start(bf16[768,384]{1,0:T(8,128)(2,1)} %w_in_ref.1) | copy-start | bytes 1769476
  2.9 22.6 %all-to-all-start = ((bf16[16,96,128]{2,1,0:T(8,128)(2,1)}), bf16[16,96,128]{2,1,0:T(8,128)(2,1)S(1)}, u32[]{:S(2)}, u32[]{:S(2)}) async-start(bf16[16,96,128]{2,1,0:T(8,128)(2,1)} %shard_map.92), calls=%async_computation | async-start | bytes 786432 | tf_op jit(solution)/shard_map/all_to_all | solution.py:287
  11.6 1.1 %copy-start.1 = (bf16[768,384]{1,0:T(8,128)(2,1)S(1)}, bf16[768,384]{1,0:T(8,128)(2,1)}, u32[]{:S(2)}) copy-start(bf16[768,384]{1,0:T(8,128)(2,1)} %w_out_ref.1) | copy-start | bytes 1769476
  34.8 3.4 %collective-permute-start.4 = (bf16[16,152,128]{2,1,0:T(8,128)(2,1)S(1)}, bf16[16,152,128]{2,1,0:T(8,128)(2,1)S(1)}, u32[]{:S(2)}, u32[]{:S(2)}) collective-permute-start(bf16[16,152,128]{2,1,0:T(8,128)(2,1)S(1)} %get-tuple-element.21), channel_id=1, source_target_pairs={{0,16},{16,0},{1,17},{17,1},{2,18},{18,2},{3,19},{19,3},{4,20},{20... | collective-permute-start | bytes 1867784 | tf_op jit(solution)/shard_map/ppermute | solution.py:274
  35.0 2.3 %collective-permute-start = (bf16[2,1,2,2,96,128]{5,4,3,2,1,0:T(8,128)(2,1)S(1)}, bf16[2,1,2,2,96,128]{5,4,3,2,1,0:T(8,128)(2,1)S(1)}, u32[]{:S(2)}, u32[]{:S(2)}) collective-permute-start(bf16[2,1,2,2,96,128]{5,4,3,2,1,0:T(8,128)(2,1)S(1)} %get-tuple-element.32), channel_id=1, source_target_pairs={{0,16},{16,0},{1,17},{17,1},{2,18},{18,2},{3,19},{19,3},{4,20},{20... | collective-permute-start | bytes 589832 | tf_op jit(solution)/shard_map/ppermute | solution.py:274
  37.3 7.4 %collective-permute-start.1 = (bf16[2,2,2,1,96,128]{5,4,3,2,1,0:T(8,128)(2,1)S(1)}, bf16[2,2,2,1,96,128]{5,4,3,2,1,0:T(8,128)(2,1)S(1)}, u32[]{:S(2)}, u32[]{:S(2)}) collective-permute-start(bf16[2,2,2,1,96,128]{5,4,3,2,1,0:T(8,128)(2,1)S(1)} %get-tuple-element.30), channel_id=1, source_target_pairs={{0,1},{1,0},{2,3},{3,2},{4,5},{5,4},{6,7},{7,6},{8,9},{9,8},{10,11... | collective-permute-start | bytes 589832 | tf_op jit(solution)/shard_map/ppermute | solution.py:274
  39.2 19.0 %all-to-all-start.1 = ((bf16[16,152,128]{2,1,0:T(8,128)(2,1)}), bf16[16,152,128]{2,1,0:T(8,128)(2,1)S(1)}, u32[]{:S(2)}, u32[]{:S(2)}) async-start(bf16[16,152,128]{2,1,0:T(8,128)(2,1)} %add_convert_fusion), calls=%async_computation.1 | async-start | bytes 1245184 | tf_op jit(solution)/shard_map/all_to_all | solution.py:308
  44.7 10.4 %collective-permute-start.2 = (bf16[2,2,1,2,96,128]{5,4,3,2,1,0:T(8,128)(2,1)S(1)}, bf16[2,2,1,2,96,128]{5,4,3,2,1,0:T(8,128)(2,1)S(1)}, u32[]{:S(2)}, u32[]{:S(2)}) collective-permute-start(bf16[2,2,1,2,96,128]{5,4,3,2,1,0:T(8,128)(2,1)S(1)} %get-tuple-element.28), channel_id=1, source_target_pairs={{0,8},{8,0},{1,9},{9,1},{2,10},{10,2},{3,11},{11,3},{4,12},{12,4},... | collective-permute-start | bytes 589832 | tf_op jit(solution)/shard_map/ppermute | solution.py:274
  55.1 10.0 %collective-permute-start.3 = (bf16[1,2,2,2,96,128]{5,4,3,2,1,0:T(8,128)(2,1)S(1)}, bf16[1,2,2,2,96,128]{5,4,3,2,1,0:T(8,128)(2,1)S(1)}, u32[]{:S(2)}, u32[]{:S(2)}) collective-permute-start(bf16[1,2,2,2,96,128]{5,4,3,2,1,0:T(8,128)(2,1)S(1)} %get-tuple-element.26), channel_id=1, source_target_pairs={{0,128},{128,0},{1,129},{129,1},{2,130},{130,2},{3,131},{131,3},{4... | collective-permute-start | bytes 589832 | tf_op jit(solution)/shard_map/ppermute | solution.py:274
  58.9 14.4 %all-to-all-start.2 = ((bf16[8,24,128]{2,1,0:T(8,128)(2,1)}), bf16[8,24,128]{2,1,0:T(8,128)(2,1)S(1)}, u32[]{:S(2)}, u32[]{:S(2)}) async-start(bf16[8,24,128]{2,1,0:T(8,128)(2,1)} %shard_map.96), calls=%async_computation.2 | async-start | bytes 98304 | tf_op jit(solution)/shard_map/all_to_all | solution.py:310

commit v3 on v2

--- a/solution.py
+++ b/solution.py
@@ -45,19 +45,25 @@
     return 8 * y1 + 4 * core + 2 * zl1 + x0
 
 
-def pack_kernel(x_hbm, g_hbm, out_ref, x_ref, g_ref, sems):
-    copies = [
-        pltpu.make_async_copy(x_hbm, x_ref, sems.at[0]),
-        pltpu.make_async_copy(g_hbm, g_ref, sems.at[1]),
-    ]
-    for copy in copies:
-        copy.start()
-    for at, ref in enumerate((x_ref, g_ref)):
-        copies[at].wait()
+def pack_kernel(x_hbm, g_hbm, out_hbm, in_ref, out_ref, in_sems, out_sems):
+    def arrive(at):
+        return pltpu.make_async_copy((x_hbm, g_hbm)[at], in_ref.at[at], in_sems.at[at])
+
+    def leave(at):
+        place = (slice(None), pl.ds(QUARTER * at, QUARTER))
+        return pltpu.make_async_copy(out_ref.at[place], out_hbm.at[place], out_sems.at[at])
+
+    arrive(0).start()
+    arrive(1).start()
+    for at in range(2):
+        arrive(at).wait()
         for t in range(4):
-            tile = ref[:, 128 * t : 128 * (t + 1)].astype(F32)
+            tile = in_ref[at, :, 128 * t : 128 * (t + 1)].astype(F32)
             for g, part in enumerate(swap_groups(quarters(tile))):
                 out_ref[4 * t + g, QUARTER * at : QUARTER * (at + 1), :] = part.astype(BF16)
+        leave(at).start()
+    leave(0).wait()
+    leave(1).wait()
 
 
 def unpack_kernel(me_ref, in_ref, f_ref, g_ref):
@@ -133,10 +139,16 @@
     return [jnp.concatenate([moved[q][t] for q in range(4)], axis=0).astype(BF16) for t in range(4)]
 
 
+def mdot(a, b):
+    n=2
+    m=a.shape[0]//n
+    return jnp.concatenate([jnp.dot(a[i*m:(i+1)*m], b, preferred_element_type=F32) for i in range(n)],axis=0)
+
+
 def main_kernel(
     me_ref, in_ref, w_ref, wt_ref,
     ret_ref, keep_ref, send_ref,
-    n_ref, nhat_ref, inv_ref, h_ref, dv_ref, gp_ref, gy_ref,
+    nt_ref, nhat_ref, inv_ref, h_ref, dv_ref, gp_ref, gyt_ref,
 ):
     me = me_ref[0]
 
@@ -170,16 +182,16 @@
         inverse = lax.rsqrt(jnp.mean(centered * centered, axis=0, keepdims=True) + 1e-05)
         nhat = centered * inverse
         normed = jnp.concatenate([nhat, ones], axis=0).astype(BF16)
-        n_ref[s] = normed
+        nt_ref[CHUNK * s : CHUNK * (s + 1), :] = normed.T
         nhat_ref[s] = nhat
         inv_ref[s] = jnp.broadcast_to(inverse, (8, CHUNK))
-        for j in range(3):
-            rows = slice(CHUNK * j, CHUNK * (j + 1))
+        for j in range(6):
+            rows = slice(128 * j, 128 * (j + 1))
             pre = jnp.dot(w_ref[rows, :WIDE], normed, preferred_element_type=F32)
             value, deriv = gelu_pair(pre)
-            h_ref[s, rows, :] = value.astype(BF16)
+            h_ref[rows, CHUNK * s : CHUNK * (s + 1)] = value.astype(BF16)
             dv_ref[s, rows, :] = deriv
-        branch = jnp.dot(wt_ref[PAIR:, :], h_ref[s], preferred_element_type=F32)
+        branch = mdot(wt_ref[PAIR:, :], h_ref[:, CHUNK * s : CHUNK * (s + 1)])
         tiles = unpair_tiles((values + branch).astype(BF16), bits[s])
     store(0, tiles, by_low)
 
@@ -188,12 +200,12 @@
         if s == 1:
             tiles = swap_tiles(tiles)
         grad_y = pair_tiles(tiles, bits[s])
-        gy_ref[s] = grad_y
-        for j in range(3):
-            rows = slice(CHUNK * j, CHUNK * (j + 1))
+        gyt_ref[CHUNK * s : CHUNK * (s + 1), :] = grad_y.T
+        for j in range(6):
+            rows = slice(128 * j, 128 * (j + 1))
             grad_pre = jnp.dot(w_ref[rows, OUT_AT:], grad_y, preferred_element_type=F32) * dv_ref[s, rows, :]
-            gp_ref[s, rows, :] = grad_pre.astype(BF16)
-        grad_norm = jnp.dot(wt_ref[:PAIR, :], gp_ref[s], preferred_element_type=F32)
+            gp_ref[rows, CHUNK * s : CHUNK * (s + 1)] = grad_pre.astype(BF16)
+        grad_norm = mdot(wt_ref[:PAIR, :], gp_ref[:, CHUNK * s : CHUNK * (s + 1)])
         nhat = nhat_ref[s]
         grad_pair = grad_y.astype(F32) + inv_ref[s, 0:1, :] * (
             grad_norm
@@ -203,20 +215,17 @@
         tiles = unpair_tiles(grad_pair.astype(BF16), bits[s])
     store(1, tiles, by_high)
 
-    def over_positions(a, b):
-        return lax.dot_general(a, b, (((1,), (1,)), ((), ())), preferred_element_type=F32)
-
     lane = lax.broadcasted_iota(jnp.int32, (8, 128), 1)
-    for j in range(4):
-        rows = slice(WIDTH * j, WIDTH * (j + 1))
-        grad_in = sum(over_positions(gp_ref[s, rows, :], n_ref[s]) for s in range(4))
-        grad_out = sum(over_positions(h_ref[s, rows, :], gy_ref[s]) for s in range(4))
-        for b in range(8):
+    for j in range(2):
+        rows = slice(PAIR * j, PAIR * (j + 1))
+        grad_in = jnp.dot(gp_ref[rows, :], nt_ref[...], preferred_element_type=F32)
+        grad_out = jnp.dot(h_ref[rows, :], gyt_ref[...], preferred_element_type=F32)
+        for b in range(16):
             at = slice(24 * b, 24 * (b + 1))
             tiles = [g[at, 128 * i : 128 * (i + 1)] for g in (grad_in, grad_out) for i in range(3)]
             thirds = [grad_in[24 * b + 8 * k : 24 * b + 8 * (k + 1), PAIR : PAIR + 1] for k in range(3)]
             extra = jnp.where(lane == 0, thirds[0], jnp.where(lane == 1, thirds[1], thirds[2]))
-            (keep_ref if j < 2 else send_ref)[8 * (j % 2) + b] = jnp.concatenate(tiles + [extra], axis=0).astype(BF16)
+            (send_ref if j else keep_ref)[b] = jnp.concatenate(tiles + [extra], axis=0).astype(BF16)
 
 
 def plane_kernel(in_ref, out_ref, total_ref):
@@ -249,7 +258,7 @@
             kernel,
             out_shape=out_shapes,
             in_specs=spec + [space or vmem] * (len(operands) - smem),
-            out_specs=jax.tree.map(lambda _: vmem, out_shapes),
+            out_specs=jax.tree.map(lambda _: space or vmem, out_shapes),
             scratch_shapes=scratch,
             compiler_params=pltpu.CompilerParams(vmem_limit_bytes=vmem_mib * MIB),
         )(*operands)
@@ -259,6 +268,24 @@
 
 def shape(*dims, dtype=BF16):
     return jax.ShapeDtypeStruct(dims, dtype)
+
+
+def run_main(me, blocks, weights, turned):
+    return call(
+        main_kernel,
+        (shape(16, 2 * QUARTER, 128), shape(16, BLOCK, 128), shape(16, BLOCK, 128)),
+        scratch=(
+            pltpu.VMEM((4 * CHUNK, WIDE), BF16),
+            pltpu.VMEM((4, PAIR, CHUNK), F32),
+            pltpu.VMEM((4, 8, CHUNK), F32),
+            pltpu.VMEM((HIDDEN, 4 * CHUNK), BF16),
+            pltpu.VMEM((4, HIDDEN, CHUNK), F32),
+            pltpu.VMEM((HIDDEN, 4 * CHUNK), BF16),
+            pltpu.VMEM((4 * CHUNK, PAIR), BF16),
+        ),
+        smem=1,
+        vmem_mib=24,
+    )(me, blocks, weights, turned)
 
 
 def give_back(blocks):
@@ -279,30 +306,23 @@
     tokens = rows * lax.axis_size(BITS)
     core = lax.axis_index("core").astype(jnp.int32).reshape(1)
     me = sum(lax.axis_index(a).astype(jnp.int32) << (3 - i) for i, a in enumerate(SECTION_GROUP)).reshape(1)
-    hbm = pl.BlockSpec(memory_space=pltpu.HBM)
-    landing = pltpu.VMEM((width, rows), BF16)
     packed = call(
-        pack_kernel, shape(16, 2 * QUARTER, 128), scratch=(landing, landing, pltpu.SemaphoreType.DMA((2,))), space=hbm, vmem_mib=60
+        pack_kernel,
+        shape(16, 2 * QUARTER, 128),
+        scratch=(
+            pltpu.VMEM((2, width, rows), BF16),
+            pltpu.VMEM((16, 2 * QUARTER, 128), BF16),
+            pltpu.SemaphoreType.DMA((2,)),
+            pltpu.SemaphoreType.DMA((2,)),
+        ),
+        space=pl.BlockSpec(memory_space=pltpu.HBM),
+        vmem_mib=60,
     )(inputs.T, upstream.T)
     blocks = lax.all_to_all(packed, SECTION_GROUP, 0, 0, tiled=True)
     ordered = call(order_kernel, (shape(HIDDEN, OUT_AT + PAIR), shape(2 * PAIR, HIDDEN)), smem=1, vmem_mib=12)(
         core, w_in, w_out, bias.reshape(1, HIDDEN)
     )
-    back, keep, send = call(
-        main_kernel,
-        (shape(16, 2 * QUARTER, 128), shape(16, BLOCK, 128), shape(16, BLOCK, 128)),
-        scratch=(
-            pltpu.VMEM((4, WIDE, CHUNK), BF16),
-            pltpu.VMEM((4, PAIR, CHUNK), F32),
-            pltpu.VMEM((4, 8, CHUNK), F32),
-            pltpu.VMEM((4, HIDDEN, CHUNK), BF16),
-            pltpu.VMEM((4, HIDDEN, CHUNK), F32),
-            pltpu.VMEM((4, HIDDEN, CHUNK), BF16),
-            pltpu.VMEM((4, PAIR, CHUNK), BF16),
-        ),
-        smem=1,
-        vmem_mib=24,
-    )(me, blocks, *ordered)
+    back, keep, send = run_main(me, blocks, *ordered)
     other = swap(send, "core")
     summed = (keep.astype(F32) + other.astype(F32)).astype(BF16)
     plane = lax.all_to_all(summed, PLANE_GROUP, 0, 0, tiled=True)

time: 74.3 us -> 73.5 us (0.989)
  Pallas kernels: 15.8 us -> 15 us
    pallas_call x6, Pallas kernels: 15.8 us -> 15 us  [run(): pl.pallas_call(kernel, out_shape=out_shapes, in_specs=spec + [space or vm...]
where the time goes in v3:
time: 73.5 us; the launch traced here: 73.1 us
  waiting for transfers between devices  30 us (41%)
  starting transfers between devices  25 us (34%)
  Pallas kernels  15 us (20%)
  other arithmetic  1.15 us (2%)
  local copies, waits for them, and re-layouts  1.1 us (1%)
  between operations  0.77 us (1%)
    pallas_call x6, Pallas kernels, run(): pl.pallas_call(kernel, out_shape=out_shapes, in_specs=spec + [space or vm...  15 us
    ppermute x5, waiting for transfers between devices, swap(): return lax.ppermute(block, axis, [(0, 1), (1, 0)])  12 us
    all_to_all x1, waiting for transfers between devices, on_device(): blocks = lax.all_to_all(packed, SECTION_GROUP, 0, 0, tiled=True)  11.2 us
    all_to_all x1, starting transfers between devices, on_device(): blocks = lax.all_to_all(packed, SECTION_GROUP, 0, 0, tiled=True)  8.66 us
    all_to_all x1, waiting for transfers between devices, on_device(): column = lax.all_to_all(columns, COLUMN_GROUP, 0, 0, tiled=True)  6.84 us
    all_to_all x1, starting transfers between devices, on_device(): column = lax.all_to_all(columns, COLUMN_GROUP, 0, 0, tiled=True)  6.21 us
    all_to_all x1, starting transfers between devices, on_device(): plane = lax.all_to_all(summed, PLANE_GROUP, 0, 0, tiled=True)  5.43 us
    ppermute x5, starting transfers between devices, swap(): return lax.ppermute(block, axis, [(0, 1), (1, 0)])  4.74 us
  transfers between devices with their start and end apart: 8, of which 4 were waited for; matrix products, arithmetic and copies ran while one was open for 2% of the time, Pallas kernels for 5%

profile of v3, /device:TPU:2, one launch (start us, length us, event | category | flops | bytes accessed | tf_op | source)
XLA Modules:
  0.0 73.1 jit_solution(17112437126357663103)
XLA Ops:
  0.6 0.0 copy-start.2
  0.6 0.0 copy-start
  0.7 2.3 %shard_map.92 = bf16[16,96,128]{2,1,0:T(8,128)(2,1)} custom-call(bf16[192,512]{1,0:T(8,128)(2,1)} %bitcast.11, bf16[192,512]{1,0:T(8,128)(2,1)} %bitcast.12), custom_call_target="tpu_custom_call" | custom-call | tf_op jit(solution)/shard_map/pallas_call | solution.py:257
  2.9 8.7 %all-to-all-start = ((bf16[16,96,128]{2,1,0:T(8,128)(2,1)}), bf16[16,96,128]{2,1,0:T(8,128)(2,1)S(1)}, u32[]{:S(2)}, u32[]{:S(2)}) async-start(bf16[16,96,128]{2,1,0:T(8,128)(2,1)} %shard_map.92), calls=%async_computation | async-start | bytes 786432 | tf_op jit(solution)/shard_map/all_to_all | solution.py:321
  11.6 0.0 copy-done.2
  11.6 0.0 copy-done
  11.6 0.0 copy-start.1
  11.6 1.1 %copy-done.1 = bf16[768,384]{1,0:T(8,128)(2,1)S(1)} copy-done((bf16[768,384]{1,0:T(8,128)(2,1)S(1)}, bf16[768,384]{1,0:T(8,128)(2,1)}, u32[]{:S(2)}) %copy-start.1) | copy-done | bytes 589848
  12.7 1.6 %shard_map.93 = (bf16[768,896]{1,0:T(8,128)(2,1)S(1)}, bf16[768,768]{1,0:T(8,128)(2,1)S(1)}) custom-call(s32[1]{0:T(128)} %bitcast.3.core_ref, bf16[768,384]{1,0:T(8,128)(2,1)S(1)} %copy-done, bf16[768,384]{1,0:T(8,128)(2,1)S(1)} %copy-done.1, f32[1,768]{1,0:T(1,128)S(1)} %reshape.30.bias_ref), custom_call_target="tpu_custom_call" | custom-call | tf_op jit(solution)/shard_map/pallas_call | solution.py:257
  14.3 11.2 %all-to-all-done.in_ref = bf16[16,96,128]{2,1,0:T(8,128)(2,1)S(1)} async-done(((bf16[16,96,128]{2,1,0:T(8,128)(2,1)}), bf16[16,96,128]{2,1,0:T(8,128)(2,1)S(1)}, u32[]{:S(2)}, u32[]{:S(2)}) %all-to-all-start) | async-done | bytes 393248 | tf_op jit(solution)/shard_map/all_to_all | solution.py:321
  25.5 8.5 %shard_map.94 = (bf16[16,96,128]{2,1,0:T(8,128)(2,1)S(1)}, bf16[16,152,128]{2,1,0:T(8,128)(2,1)S(1)}, bf16[16,152,128]{2,1,0:T(8,128)(2,1)S(1)}) custom-call(s32[1]{0:T(128)} %bitcast.me_ref, bf16[16,96,128]{2,1,0:T(8,128)(2,1)S(1)} %all-to-all-done.in_ref, bf16[768,896]{1,0:T(8,128)(2,1)S(1)} %get-tuple-element.15.w_ref, ...), custom_call_target="tpu_custom_call" | custom-call | tf_op jit(solution)/shard_map/pallas_call | solution.py:257
  34.0 0.1 collective-permute-start.4
  34.1 0.6 collective-permute-start
  34.7 1.7 %collective-permute-done = bf16[2,1,2,2,96,128]{5,4,3,2,1,0:T(8,128)(2,1)S(1)} collective-permute-done((bf16[2,1,2,2,96,128]{5,4,3,2,1,0:T(8,128)(2,1)S(1)}, bf16[2,1,2,2,96,128]{5,4,3,2,1,0:T(8,128)(2,1)S(1)}, u32[]{:S(2)}, u32[]{:S(2)}) %collective-permute-start) | collective-permute-done | bytes 196640 | tf_op jit(solution)/shard_map/ppermute | solution.py:301
  36.4 0.9 %collective-permute-start.1 = (bf16[2,2,2,1,96,128]{5,4,3,2,1,0:T(8,128)(2,1)S(1)}, bf16[2,2,2,1,96,128]{5,4,3,2,1,0:T(8,128)(2,1)S(1)}, u32[]{:S(2)}, u32[]{:S(2)}) collective-permute-start(bf16[2,2,2,1,96,128]{5,4,3,2,1,0:T(8,128)(2,1)S(1)} %get-tuple-element.30), channel_id=1, source_target_pairs={{0,1},{1,0},{2,3},{3,2},{4,5},{5,4},{6,7},{7,6},{8,9},{9,8},{10,11... | collective-permute-start | bytes 589832 | tf_op jit(solution)/shard_map/ppermute | solution.py:301
  37.4 0.0 collective-permute-done.4
  37.4 1.0 %add_convert_fusion = bf16[16,152,128]{2,1,0:T(8,128)(2,1)} fusion(bf16[16,152,128]{2,1,0:T(8,128)(2,1)S(1)} %collective-permute-done.4, bf16[16,152,128]{2,1,0:T(8,128)(2,1)S(1)} %get-tuple-element.20), kind=kLoop, calls=%fused_computation | loop fusion | flops 1245184 | bytes 1867776 | tf_op jit(solution)/shard_map/convert_element_type | solution.py:327
  38.4 5.4 %all-to-all-start.1 = ((bf16[16,152,128]{2,1,0:T(8,128)(2,1)}), bf16[16,152,128]{2,1,0:T(8,128)(2,1)S(1)}, u32[]{:S(2)}, u32[]{:S(2)}) async-start(bf16[16,152,128]{2,1,0:T(8,128)(2,1)} %add_convert_fusion), calls=%async_computation.1 | async-start | bytes 1245184 | tf_op jit(solution)/shard_map/all_to_all | solution.py:328
  43.8 0.0 collective-permute-done.1
  43.8 0.1 collective-permute-start.2
  43.9 10.3 %collective-permute-done.2 = bf16[2,2,1,2,96,128]{5,4,3,2,1,0:T(8,128)(2,1)S(1)} collective-permute-done((bf16[2,2,1,2,96,128]{5,4,3,2,1,0:T(8,128)(2,1)S(1)}, bf16[2,2,1,2,96,128]{5,4,3,2,1,0:T(8,128)(2,1)S(1)}, u32[]{:S(2)}, u32[]{:S(2)}) %collective-permute-start.2) | collective-permute-done | bytes 196640 | tf_op jit(solution)/shard_map/ppermute | solution.py:301
  54.3 3.1 %collective-permute-start.3 = (bf16[1,2,2,2,96,128]{5,4,3,2,1,0:T(8,128)(2,1)S(1)}, bf16[1,2,2,2,96,128]{5,4,3,2,1,0:T(8,128)(2,1)S(1)}, u32[]{:S(2)}, u32[]{:S(2)}) collective-permute-start(bf16[1,2,2,2,96,128]{5,4,3,2,1,0:T(8,128)(2,1)S(1)} %get-tuple-element.26), channel_id=1, source_target_pairs={{0,128},{128,0},{1,129},{129,1},{2,130},{130,2},{3,131},{131,3},{4... | collective-permute-start | bytes 589832 | tf_op jit(solution)/shard_map/ppermute | solution.py:301
  57.3 0.0 all-to-all-done.1.in_ref
  57.3 0.7 shard_map.96
  58.0 6.2 %all-to-all-start.2 = ((bf16[8,24,128]{2,1,0:T(8,128)(2,1)}), bf16[8,24,128]{2,1,0:T(8,128)(2,1)S(1)}, u32[]{:S(2)}, u32[]{:S(2)}) async-start(bf16[8,24,128]{2,1,0:T(8,128)(2,1)} %shard_map.96), calls=%async_computation.2 | async-start | bytes 98304 | tf_op jit(solution)/shard_map/all_to_all | solution.py:330
  64.3 0.0 collective-permute-done.3
  64.3 1.3 %shard_map.95 = (bf16[192,512]{1,0:T(8,128)(2,1)}, bf16[192,512]{1,0:T(8,128)(2,1)}) custom-call(s32[1]{0:T(128)} %bitcast.me_ref, bf16[16,96,128]{2,1,0:T(8,128)(2,1)S(1)} %bitcast.9), custom_call_target="tpu_custom_call" | custom-call | tf_op jit(solution)/shard_map/pallas_call | solution.py:257
  65.6 6.8 %all-to-all-done.2.in_ref = bf16[8,24,128]{2,1,0:T(8,128)(2,1)S(1)} async-done(((bf16[8,24,128]{2,1,0:T(8,128)(2,1)}), bf16[8,24,128]{2,1,0:T(8,128)(2,1)S(1)}, u32[]{:S(2)}, u32[]{:S(2)}) %all-to-all-start.2) | async-done | bytes 49184 | tf_op jit(solution)/shard_map/all_to_all | solution.py:330
  72.5 0.6 shard_map.97
  (6 shorter events, 0.2 us)
Async XLA Ops:
  0.6 10.9 %copy-start.2 = (f32[768]{0:T(1024)S(1)}, f32[768]{0:T(1024)}, u32[]{:S(2)}) copy-start(f32[768]{0:T(1024)} %param.9) | copy-start | bytes 9220
  0.6 11.0 %copy-start = (bf16[768,384]{1,0:T(8,128)(2,1)S(1)}, bf16[768,384]{1,0:T(8,128)(2,1)}, u32[]{:S(2)}) copy-start(bf16[768,384]{1,0:T(8,128)(2,1)} %w_in_ref.1) | copy-start | bytes 1769476
  2.9 22.6 %all-to-all-start = ((bf16[16,96,128]{2,1,0:T(8,128)(2,1)}), bf16[16,96,128]{2,1,0:T(8,128)(2,1)S(1)}, u32[]{:S(2)}, u32[]{:S(2)}) async-start(bf16[16,96,128]{2,1,0:T(8,128)(2,1)} %shard_map.92), calls=%async_computation | async-start | bytes 786432 | tf_op jit(solution)/shard_map/all_to_all | solution.py:321
  11.6 1.1 %copy-start.1 = (bf16[768,384]{1,0:T(8,128)(2,1)S(1)}, bf16[768,384]{1,0:T(8,128)(2,1)}, u32[]{:S(2)}) copy-start(bf16[768,384]{1,0:T(8,128)(2,1)} %w_out_ref.1) | copy-start | bytes 1769476
  34.0 3.4 %collective-permute-start.4 = (bf16[16,152,128]{2,1,0:T(8,128)(2,1)S(1)}, bf16[16,152,128]{2,1,0:T(8,128)(2,1)S(1)}, u32[]{:S(2)}, u32[]{:S(2)}) collective-permute-start(bf16[16,152,128]{2,1,0:T(8,128)(2,1)S(1)} %get-tuple-element.21), channel_id=1, source_target_pairs={{0,16},{16,0},{1,17},{17,1},{2,18},{18,2},{3,19},{19,3},{4,20},{20... | collective-permute-start | bytes 1867784 | tf_op jit(solution)/shard_map/ppermute | solution.py:301
  34.1 2.3 %collective-permute-start = (bf16[2,1,2,2,96,128]{5,4,3,2,1,0:T(8,128)(2,1)S(1)}, bf16[2,1,2,2,96,128]{5,4,3,2,1,0:T(8,128)(2,1)S(1)}, u32[]{:S(2)}, u32[]{:S(2)}) collective-permute-start(bf16[2,1,2,2,96,128]{5,4,3,2,1,0:T(8,128)(2,1)S(1)} %get-tuple-element.32), channel_id=1, source_target_pairs={{0,16},{16,0},{1,17},{17,1},{2,18},{18,2},{3,19},{19,3},{4,20},{20... | collective-permute-start | bytes 589832 | tf_op jit(solution)/shard_map/ppermute | solution.py:301
  36.4 7.4 %collective-permute-start.1 = (bf16[2,2,2,1,96,128]{5,4,3,2,1,0:T(8,128)(2,1)S(1)}, bf16[2,2,2,1,96,128]{5,4,3,2,1,0:T(8,128)(2,1)S(1)}, u32[]{:S(2)}, u32[]{:S(2)}) collective-permute-start(bf16[2,2,2,1,96,128]{5,4,3,2,1,0:T(8,128)(2,1)S(1)} %get-tuple-element.30), channel_id=1, source_target_pairs={{0,1},{1,0},{2,3},{3,2},{4,5},{5,4},{6,7},{7,6},{8,9},{9,8},{10,11... | collective-permute-start | bytes 589832 | tf_op jit(solution)/shard_map/ppermute | solution.py:301
  38.4 19.0 %all-to-all-start.1 = ((bf16[16,152,128]{2,1,0:T(8,128)(2,1)}), bf16[16,152,128]{2,1,0:T(8,128)(2,1)S(1)}, u32[]{:S(2)}, u32[]{:S(2)}) async-start(bf16[16,152,128]{2,1,0:T(8,128)(2,1)} %add_convert_fusion), calls=%async_computation.1 | async-start | bytes 1245184 | tf_op jit(solution)/shard_map/all_to_all | solution.py:328
  43.8 10.4 %collective-permute-start.2 = (bf16[2,2,1,2,96,128]{5,4,3,2,1,0:T(8,128)(2,1)S(1)}, bf16[2,2,1,2,96,128]{5,4,3,2,1,0:T(8,128)(2,1)S(1)}, u32[]{:S(2)}, u32[]{:S(2)}) collective-permute-start(bf16[2,2,1,2,96,128]{5,4,3,2,1,0:T(8,128)(2,1)S(1)} %get-tuple-element.28), channel_id=1, source_target_pairs={{0,8},{8,0},{1,9},{9,1},{2,10},{10,2},{3,11},{11,3},{4,12},{12,4},... | collective-permute-start | bytes 589832 | tf_op jit(solution)/shard_map/ppermute | solution.py:301
  54.3 10.0 %collective-permute-start.3 = (bf16[1,2,2,2,96,128]{5,4,3,2,1,0:T(8,128)(2,1)S(1)}, bf16[1,2,2,2,96,128]{5,4,3,2,1,0:T(8,128)(2,1)S(1)}, u32[]{:S(2)}, u32[]{:S(2)}) collective-permute-start(bf16[1,2,2,2,96,128]{5,4,3,2,1,0:T(8,128)(2,1)S(1)} %get-tuple-element.26), channel_id=1, source_target_pairs={{0,128},{128,0},{1,129},{129,1},{2,130},{130,2},{3,131},{131,3},{4... | collective-permute-start | bytes 589832 | tf_op jit(solution)/shard_map/ppermute | solution.py:301
  58.0 14.4 %all-to-all-start.2 = ((bf16[8,24,128]{2,1,0:T(8,128)(2,1)}), bf16[8,24,128]{2,1,0:T(8,128)(2,1)S(1)}, u32[]{:S(2)}, u32[]{:S(2)}) async-start(bf16[8,24,128]{2,1,0:T(8,128)(2,1)} %shard_map.96), calls=%async_computation.2 | async-start | bytes 98304 | tf_op jit(solution)/shard_map/all_to_all | solution.py:330

commit v4 on v3

--- a/solution.py
+++ b/solution.py
@@ -31,8 +31,12 @@
         for i in range(4):
             if not i & stride:
                 a, b = parts[i], parts[i | stride]
-                out[i] = jnp.where(low, a, pltpu.roll(b, at, 1))
-                out[i | stride] = jnp.where(low, pltpu.roll(a, 128 - at, 1), b)
+                if at == 64:
+                    crossed = pltpu.roll(jnp.where(low, b, a), at, 1)
+                    out[i], out[i | stride] = jnp.where(low, a, crossed), jnp.where(low, crossed, b)
+                else:
+                    out[i] = jnp.where(low, a, pltpu.roll(b, at, 1))
+                    out[i | stride] = jnp.where(low, pltpu.roll(a, 128 - at, 1), b)
         parts = out
     return parts
 

time: 73.5 us -> 73.4 us (level)
  no operation moved by 1% of the time
where the time goes in v4:
time: 73.4 us; the launch traced here: 73 us
  waiting for transfers between devices  30.2 us (41%)
  starting transfers between devices  25 us (34%)
  Pallas kernels  14.7 us (20%)
  other arithmetic  1.15 us (2%)
  local copies, waits for them, and re-layouts  1.1 us (1%)
  between operations  0.77 us (1%)
    pallas_call x6, Pallas kernels, run(): pl.pallas_call(kernel, out_shape=out_shapes, in_specs=spec + [space or vm...  14.7 us
    ppermute x5, waiting for transfers between devices, swap(): return lax.ppermute(block, axis, [(0, 1), (1, 0)])  12 us
    all_to_all x1, waiting for transfers between devices, on_device(): blocks = lax.all_to_all(packed, SECTION_GROUP, 0, 0, tiled=True)  11.2 us
    all_to_all x1, starting transfers between devices, on_device(): blocks = lax.all_to_all(packed, SECTION_GROUP, 0, 0, tiled=True)  8.66 us
    all_to_all x1, waiting for transfers between devices, on_device(): column = lax.all_to_all(columns, COLUMN_GROUP, 0, 0, tiled=True)  7 us
    all_to_all x1, starting transfers between devices, on_device(): column = lax.all_to_all(columns, COLUMN_GROUP, 0, 0, tiled=True)  6.21 us
    all_to_all x1, starting transfers between devices, on_device(): plane = lax.all_to_all(summed, PLANE_GROUP, 0, 0, tiled=True)  5.42 us
    ppermute x5, starting transfers between devices, swap(): return lax.ppermute(block, axis, [(0, 1), (1, 0)])  4.74 us
  transfers between devices with their start and end apart: 8, of which 4 were waited for; matrix products, arithmetic and copies ran while one was open for 2% of the time, Pallas kernels for 5%

profile of v4, /device:TPU:2, one launch (start us, length us, event | category | flops | bytes accessed | tf_op | source)
XLA Modules:
  0.0 73.0 jit_solution(16661004350053386053)
XLA Ops:
  0.6 0.0 copy-start.2
  0.6 0.0 copy-start
  0.7 2.1 %shard_map.92 = bf16[16,96,128]{2,1,0:T(8,128)(2,1)} custom-call(bf16[192,512]{1,0:T(8,128)(2,1)} %bitcast.11, bf16[192,512]{1,0:T(8,128)(2,1)} %bitcast.12), custom_call_target="tpu_custom_call" | custom-call | tf_op jit(solution)/shard_map/pallas_call | solution.py:261
  2.8 8.7 %all-to-all-start = ((bf16[16,96,128]{2,1,0:T(8,128)(2,1)}), bf16[16,96,128]{2,1,0:T(8,128)(2,1)S(1)}, u32[]{:S(2)}, u32[]{:S(2)}) async-start(bf16[16,96,128]{2,1,0:T(8,128)(2,1)} %shard_map.92), calls=%async_computation | async-start | bytes 786432 | tf_op jit(solution)/shard_map/all_to_all | solution.py:325
  11.5 0.0 copy-done.2
  11.5 0.0 copy-done
  11.5 0.0 copy-start.1
  11.5 1.1 %copy-done.1 = bf16[768,384]{1,0:T(8,128)(2,1)S(1)} copy-done((bf16[768,384]{1,0:T(8,128)(2,1)S(1)}, bf16[768,384]{1,0:T(8,128)(2,1)}, u32[]{:S(2)}) %copy-start.1) | copy-done | bytes 589848
  12.6 1.6 %shard_map.93 = (bf16[768,896]{1,0:T(8,128)(2,1)S(1)}, bf16[768,768]{1,0:T(8,128)(2,1)S(1)}) custom-call(s32[1]{0:T(128)} %bitcast.3.core_ref, bf16[768,384]{1,0:T(8,128)(2,1)S(1)} %copy-done, bf16[768,384]{1,0:T(8,128)(2,1)S(1)} %copy-done.1, f32[1,768]{1,0:T(1,128)S(1)} %reshape.30.bias_ref), custom_call_target="tpu_custom_call" | custom-call | tf_op jit(solution)/shard_map/pallas_call | solution.py:261
  14.2 11.2 %all-to-all-done.in_ref = bf16[16,96,128]{2,1,0:T(8,128)(2,1)S(1)} async-done(((bf16[16,96,128]{2,1,0:T(8,128)(2,1)}), bf16[16,96,128]{2,1,0:T(8,128)(2,1)S(1)}, u32[]{:S(2)}, u32[]{:S(2)}) %all-to-all-start) | async-done | bytes 393248 | tf_op jit(solution)/shard_map/all_to_all | solution.py:325
  25.4 8.5 %shard_map.94 = (bf16[16,96,128]{2,1,0:T(8,128)(2,1)S(1)}, bf16[16,152,128]{2,1,0:T(8,128)(2,1)S(1)}, bf16[16,152,128]{2,1,0:T(8,128)(2,1)S(1)}) custom-call(s32[1]{0:T(128)} %bitcast.me_ref, bf16[16,96,128]{2,1,0:T(8,128)(2,1)S(1)} %all-to-all-done.in_ref, bf16[768,896]{1,0:T(8,128)(2,1)S(1)} %get-tuple-element.15.w_ref, ...), custom_call_target="tpu_custom_call" | custom-call | tf_op jit(solution)/shard_map/pallas_call | solution.py:261
  33.9 0.1 collective-permute-start.4
  34.0 0.6 collective-permute-start
  34.6 1.7 %collective-permute-done = bf16[2,1,2,2,96,128]{5,4,3,2,1,0:T(8,128)(2,1)S(1)} collective-permute-done((bf16[2,1,2,2,96,128]{5,4,3,2,1,0:T(8,128)(2,1)S(1)}, bf16[2,1,2,2,96,128]{5,4,3,2,1,0:T(8,128)(2,1)S(1)}, u32[]{:S(2)}, u32[]{:S(2)}) %collective-permute-start) | collective-permute-done | bytes 196640 | tf_op jit(solution)/shard_map/ppermute | solution.py:305
  36.3 0.9 %collective-permute-start.1 = (bf16[2,2,2,1,96,128]{5,4,3,2,1,0:T(8,128)(2,1)S(1)}, bf16[2,2,2,1,96,128]{5,4,3,2,1,0:T(8,128)(2,1)S(1)}, u32[]{:S(2)}, u32[]{:S(2)}) collective-permute-start(bf16[2,2,2,1,96,128]{5,4,3,2,1,0:T(8,128)(2,1)S(1)} %get-tuple-element.30), channel_id=1, source_target_pairs={{0,1},{1,0},{2,3},{3,2},{4,5},{5,4},{6,7},{7,6},{8,9},{9,8},{10,11... | collective-permute-start | bytes 589832 | tf_op jit(solution)/shard_map/ppermute | solution.py:305
  37.2 0.0 collective-permute-done.4
  37.2 1.0 %add_convert_fusion = bf16[16,152,128]{2,1,0:T(8,128)(2,1)} fusion(bf16[16,152,128]{2,1,0:T(8,128)(2,1)S(1)} %collective-permute-done.4, bf16[16,152,128]{2,1,0:T(8,128)(2,1)S(1)} %get-tuple-element.20), kind=kLoop, calls=%fused_computation | loop fusion | flops 1245184 | bytes 1867776 | tf_op jit(solution)/shard_map/convert_element_type | solution.py:331
  38.3 5.4 %all-to-all-start.1 = ((bf16[16,152,128]{2,1,0:T(8,128)(2,1)}), bf16[16,152,128]{2,1,0:T(8,128)(2,1)S(1)}, u32[]{:S(2)}, u32[]{:S(2)}) async-start(bf16[16,152,128]{2,1,0:T(8,128)(2,1)} %add_convert_fusion), calls=%async_computation.1 | async-start | bytes 1245184 | tf_op jit(solution)/shard_map/all_to_all | solution.py:332
  43.7 0.0 collective-permute-done.1
  43.7 0.1 collective-permute-start.2
  43.8 10.3 %collective-permute-done.2 = bf16[2,2,1,2,96,128]{5,4,3,2,1,0:T(8,128)(2,1)S(1)} collective-permute-done((bf16[2,2,1,2,96,128]{5,4,3,2,1,0:T(8,128)(2,1)S(1)}, bf16[2,2,1,2,96,128]{5,4,3,2,1,0:T(8,128)(2,1)S(1)}, u32[]{:S(2)}, u32[]{:S(2)}) %collective-permute-start.2) | collective-permute-done | bytes 196640 | tf_op jit(solution)/shard_map/ppermute | solution.py:305
  54.2 3.1 %collective-permute-start.3 = (bf16[1,2,2,2,96,128]{5,4,3,2,1,0:T(8,128)(2,1)S(1)}, bf16[1,2,2,2,96,128]{5,4,3,2,1,0:T(8,128)(2,1)S(1)}, u32[]{:S(2)}, u32[]{:S(2)}) collective-permute-start(bf16[1,2,2,2,96,128]{5,4,3,2,1,0:T(8,128)(2,1)S(1)} %get-tuple-element.26), channel_id=1, source_target_pairs={{0,128},{128,0},{1,129},{129,1},{2,130},{130,2},{3,131},{131,3},{4... | collective-permute-start | bytes 589832 | tf_op jit(solution)/shard_map/ppermute | solution.py:305
  57.2 0.0 all-to-all-done.1.in_ref
  57.2 0.7 shard_map.96
  57.9 6.2 %all-to-all-start.2 = ((bf16[8,24,128]{2,1,0:T(8,128)(2,1)}), bf16[8,24,128]{2,1,0:T(8,128)(2,1)S(1)}, u32[]{:S(2)}, u32[]{:S(2)}) async-start(bf16[8,24,128]{2,1,0:T(8,128)(2,1)} %shard_map.96), calls=%async_computation.2 | async-start | bytes 98304 | tf_op jit(solution)/shard_map/all_to_all | solution.py:334
  64.2 0.0 collective-permute-done.3
  64.2 1.1 %shard_map.95 = (bf16[192,512]{1,0:T(8,128)(2,1)}, bf16[192,512]{1,0:T(8,128)(2,1)}) custom-call(s32[1]{0:T(128)} %bitcast.me_ref, bf16[16,96,128]{2,1,0:T(8,128)(2,1)S(1)} %bitcast.9), custom_call_target="tpu_custom_call" | custom-call | tf_op jit(solution)/shard_map/pallas_call | solution.py:261
  65.4 7.0 %all-to-all-done.2.in_ref = bf16[8,24,128]{2,1,0:T(8,128)(2,1)S(1)} async-done(((bf16[8,24,128]{2,1,0:T(8,128)(2,1)}), bf16[8,24,128]{2,1,0:T(8,128)(2,1)S(1)}, u32[]{:S(2)}, u32[]{:S(2)}) %all-to-all-start.2) | async-done | bytes 49184 | tf_op jit(solution)/shard_map/all_to_all | solution.py:334
  72.4 0.6 shard_map.97
  (6 shorter events, 0.2 us)
Async XLA Ops:
  0.6 10.8 %copy-start.2 = (f32[768]{0:T(1024)S(1)}, f32[768]{0:T(1024)}, u32[]{:S(2)}) copy-start(f32[768]{0:T(1024)} %param.9) | copy-start | bytes 9220
  0.6 10.9 %copy-start = (bf16[768,384]{1,0:T(8,128)(2,1)S(1)}, bf16[768,384]{1,0:T(8,128)(2,1)}, u32[]{:S(2)}) copy-start(bf16[768,384]{1,0:T(8,128)(2,1)} %w_in_ref.1) | copy-start | bytes 1769476
  2.8 22.6 %all-to-all-start = ((bf16[16,96,128]{2,1,0:T(8,128)(2,1)}), bf16[16,96,128]{2,1,0:T(8,128)(2,1)S(1)}, u32[]{:S(2)}, u32[]{:S(2)}) async-start(bf16[16,96,128]{2,1,0:T(8,128)(2,1)} %shard_map.92), calls=%async_computation | async-start | bytes 786432 | tf_op jit(solution)/shard_map/all_to_all | solution.py:325
  11.5 1.1 %copy-start.1 = (bf16[768,384]{1,0:T(8,128)(2,1)S(1)}, bf16[768,384]{1,0:T(8,128)(2,1)}, u32[]{:S(2)}) copy-start(bf16[768,384]{1,0:T(8,128)(2,1)} %w_out_ref.1) | copy-start | bytes 1769476
  33.9 3.4 %collective-permute-start.4 = (bf16[16,152,128]{2,1,0:T(8,128)(2,1)S(1)}, bf16[16,152,128]{2,1,0:T(8,128)(2,1)S(1)}, u32[]{:S(2)}, u32[]{:S(2)}) collective-permute-start(bf16[16,152,128]{2,1,0:T(8,128)(2,1)S(1)} %get-tuple-element.21), channel_id=1, source_target_pairs={{0,16},{16,0},{1,17},{17,1},{2,18},{18,2},{3,19},{19,3},{4,20},{20... | collective-permute-start | bytes 1867784 | tf_op jit(solution)/shard_map/ppermute | solution.py:305
  34.0 2.3 %collective-permute-start = (bf16[2,1,2,2,96,128]{5,4,3,2,1,0:T(8,128)(2,1)S(1)}, bf16[2,1,2,2,96,128]{5,4,3,2,1,0:T(8,128)(2,1)S(1)}, u32[]{:S(2)}, u32[]{:S(2)}) collective-permute-start(bf16[2,1,2,2,96,128]{5,4,3,2,1,0:T(8,128)(2,1)S(1)} %get-tuple-element.32), channel_id=1, source_target_pairs={{0,16},{16,0},{1,17},{17,1},{2,18},{18,2},{3,19},{19,3},{4,20},{20... | collective-permute-start | bytes 589832 | tf_op jit(solution)/shard_map/ppermute | solution.py:305
  36.3 7.4 %collective-permute-start.1 = (bf16[2,2,2,1,96,128]{5,4,3,2,1,0:T(8,128)(2,1)S(1)}, bf16[2,2,2,1,96,128]{5,4,3,2,1,0:T(8,128)(2,1)S(1)}, u32[]{:S(2)}, u32[]{:S(2)}) collective-permute-start(bf16[2,2,2,1,96,128]{5,4,3,2,1,0:T(8,128)(2,1)S(1)} %get-tuple-element.30), channel_id=1, source_target_pairs={{0,1},{1,0},{2,3},{3,2},{4,5},{5,4},{6,7},{7,6},{8,9},{9,8},{10,11... | collective-permute-start | bytes 589832 | tf_op jit(solution)/shard_map/ppermute | solution.py:305
  38.3 19.0 %all-to-all-start.1 = ((bf16[16,152,128]{2,1,0:T(8,128)(2,1)}), bf16[16,152,128]{2,1,0:T(8,128)(2,1)S(1)}, u32[]{:S(2)}, u32[]{:S(2)}) async-start(bf16[16,152,128]{2,1,0:T(8,128)(2,1)} %add_convert_fusion), calls=%async_computation.1 | async-start | bytes 1245184 | tf_op jit(solution)/shard_map/all_to_all | solution.py:332
  43.7 10.4 %collective-permute-start.2 = (bf16[2,2,1,2,96,128]{5,4,3,2,1,0:T(8,128)(2,1)S(1)}, bf16[2,2,1,2,96,128]{5,4,3,2,1,0:T(8,128)(2,1)S(1)}, u32[]{:S(2)}, u32[]{:S(2)}) collective-permute-start(bf16[2,2,1,2,96,128]{5,4,3,2,1,0:T(8,128)(2,1)S(1)} %get-tuple-element.28), channel_id=1, source_target_pairs={{0,8},{8,0},{1,9},{9,1},{2,10},{10,2},{3,11},{11,3},{4,12},{12,4},... | collective-permute-start | bytes 589832 | tf_op jit(solution)/shard_map/ppermute | solution.py:305
  54.2 10.0 %collective-permute-start.3 = (bf16[1,2,2,2,96,128]{5,4,3,2,1,0:T(8,128)(2,1)S(1)}, bf16[1,2,2,2,96,128]{5,4,3,2,1,0:T(8,128)(2,1)S(1)}, u32[]{:S(2)}, u32[]{:S(2)}) collective-permute-start(bf16[1,2,2,2,96,128]{5,4,3,2,1,0:T(8,128)(2,1)S(1)} %get-tuple-element.26), channel_id=1, source_target_pairs={{0,128},{128,0},{1,129},{129,1},{2,130},{130,2},{3,131},{131,3},{4... | collective-permute-start | bytes 589832 | tf_op jit(solution)/shard_map/ppermute | solution.py:305
  57.9 14.4 %all-to-all-start.2 = ((bf16[8,24,128]{2,1,0:T(8,128)(2,1)}), bf16[8,24,128]{2,1,0:T(8,128)(2,1)S(1)}, u32[]{:S(2)}, u32[]{:S(2)}) async-start(bf16[8,24,128]{2,1,0:T(8,128)(2,1)} %shard_map.96), calls=%async_computation.2 | async-start | bytes 98304 | tf_op jit(solution)/shard_map/all_to_all | solution.py:334
